TPU v7x, 32 devices: a whole 2x2x4 slice. The times are simulated.
32 devices in a mesh: tower: 2 (over x), batch: 16 (over z, y, core).
Axes of the slice: x: 2, y: 2, z: 4, core: 2. Of those that a mesh axis runs over, the one named last changes fastest.
Arguments:
- hidden_in: bfloat16 [2, 2, 8192, 768], P(None, 'tower', 'batch'), may hold values from -6 to 6
- query_lengths: int32 [2, 272], P(None, 'batch'), may hold values from 4 to 30, as said below
- passage_lengths: int32 [2, 32], P(None, 'batch'), may hold values from 20 to 200, as said below
- positives: int32 [2, 272], P(None, 'batch'), may hold values from 0 to 31
- query_weight: bfloat16 [768, 768], P(('tower', 'batch')), may hold values from -0.21875 to 0.21875
- query_bias: bfloat16 [768], P(('tower', 'batch')), may hold values from -3 to 3
- key_weight: bfloat16 [768, 768], P(('tower', 'batch')), may hold values from -0.21875 to 0.21875
- value_weight: bfloat16 [768, 768], P(('tower', 'batch')), may hold values from -0.21875 to 0.21875
- value_bias: bfloat16 [768], P(('tower', 'batch')), may hold values from -3 to 3
- output_weight: bfloat16 [768, 768], P(('tower', 'batch')), may hold values from -1.25 to 1.25
- output_bias: bfloat16 [768], P(('tower', 'batch')), may hold values from -3 to 3
- first_gain: bfloat16 [768], P(('tower', 'batch')), may hold values from 0.5 to 1.5
- first_shift: bfloat16 [768], P(('tower', 'batch')), may hold values from -2 to 2
- inner_weight: bfloat16 [768, 3072], P(('tower', 'batch')), may hold values from -0.21875 to 0.21875
- inner_bias: bfloat16 [3072], P(('tower', 'batch')), may hold values from -3 to 3
- outer_weight: bfloat16 [3072, 768], P(('tower', 'batch')), may hold values from -0.109375 to 0.109375
- outer_bias: bfloat16 [768], P(('tower', 'batch')), may hold values from -3 to 3
- second_gain: bfloat16 [768], P(('tower', 'batch')), may hold values from 0.5 to 1.5
- second_shift: bfloat16 [768], P(('tower', 'batch')), may hold values from -2 to 2
Outputs:
- hidden_out: bfloat16 [2, 2, 8192, 768], P(None, 'tower', 'batch')
- input_grad: bfloat16 [2, 2, 8192, 768], P(None, 'tower', 'batch')
- query_weight_grad: float32 [768, 768], P(('tower', 'batch'))
- query_bias_grad: float32 [768], P(('tower', 'batch'))
- key_weight_grad: float32 [768, 768], P(('tower', 'batch'))
- value_weight_grad: float32 [768, 768], P(('tower', 'batch'))
- value_bias_grad: float32 [768], P(('tower', 'batch'))
- output_weight_grad: float32 [768, 768], P(('tower', 'batch'))
- output_bias_grad: float32 [768], P(('tower', 'batch'))
- first_gain_grad: float32 [768], P(('tower', 'batch'))
- first_shift_grad: float32 [768], P(('tower', 'batch'))
- inner_weight_grad: float32 [768, 3072], P(('tower', 'batch'))
- inner_bias_grad: float32 [3072], P(('tower', 'batch'))
- outer_weight_grad: float32 [3072, 768], P(('tower', 'batch'))
- outer_bias_grad: float32 [768], P(('tower', 'batch'))
- second_gain_grad: float32 [768], P(('tower', 'batch'))
- second_shift_grad: float32 [768], P(('tower', 'batch'))
Inputs may be any that keep to these rules, and one draw needn't show every extreme that they name: `query_lengths`: within each block of 17 consecutive lengths (one stream) exactly one is 30; each block sums to at most 512. `passage_lengths`: within each block of 2 consecutive lengths (one stream) exactly one is 200; each block sums to at most 512.
All inputs are finite; a program needn't handle non-finite values.
Results may differ from a plain program's by a relative error of at most 0.034.
Values may be sent and summed in bfloat16 or wider, within the bound.
A program may use at most 192 MiB of HBM per device.

v0:
```python
import jax
import jax.numpy as jnp
from jax import lax
from jax.sharding import PartitionSpec as P

HEADS = 12


EPSILON = 1e-12
MASKED = -1e30


def partner_2(x, axis, apart):
    return lax.ppermute(x, axis, [(i, i ^ 1 << apart) for i in range(lax.axis_size(axis))])


def as_sent(x):
    return jax.tree.map(lambda a: a.astype(jnp.bfloat16) if a.dtype == jnp.float32 else a, x)


def product(left, right):
    return jnp.dot(left, right, preferred_element_type=jnp.float32)


def product_tn(left, right):
    return jnp.einsum("ta,tb->ab", left, right, preferred_element_type=jnp.float32)


def product_nt(left, right):
    return jnp.einsum("ra,ba->rb", left, right, preferred_element_type=jnp.float32)


def normalize(values, gains, shifts):
    average = jnp.mean(values, -1, keepdims=True)
    centred = values - average
    inverse = lax.rsqrt(jnp.mean(centred * centred, -1, keepdims=True) + EPSILON)
    normed = centred * inverse
    return (normed * gains + shifts, normed, inverse)


def normalize_back(upstream, normed, inverse, gains):
    scaled = upstream * gains
    inner = (
        scaled
        - jnp.mean(scaled, -1, keepdims=True)
        - normed * jnp.mean(scaled * normed, -1, keepdims=True)
    )
    return (inner * inverse, jnp.sum(upstream * normed, 0), jnp.sum(upstream, 0))


def gelu_slope(values):
    return (
        0.5 * (1.0 + lax.erf(values * 0.7071067811865476))
        + values * jnp.exp(-0.5 * values * values) * 0.3989422804014327
    )


def segments(lengths, token_rows):
    ends = jnp.cumsum(lengths)
    places = jnp.arange(token_rows, dtype=jnp.int32)
    labels = jnp.sum((places[:, None] >= ends[None, :]).astype(jnp.int32), 1)
    starts = jnp.minimum(ends - lengths, token_rows - 1)
    return (labels, places < ends[-1], starts, lengths > 0)


def tail(inputs, attended, params):
    out_mat, out_vec, gain_one, shift_one = (params[5], params[6], params[7], params[8])
    inner_mat, inner_vec, outer_mat, outer_vec, gain_two, shift_two = params[9:15]
    branch = product(attended, out_mat) + out_vec
    hidden_full, normed_one, inverse_one = normalize(
        inputs.astype(jnp.float32) + branch, gain_one, shift_one
    )
    hidden_low = hidden_full.astype(jnp.bfloat16)
    inner = product(hidden_low, inner_mat) + inner_vec
    active = jax.nn.gelu(inner, approximate=False).astype(jnp.bfloat16)
    outer = product(active, outer_mat) + outer_vec
    result, normed_two, inverse_two = normalize(
        hidden_low.astype(jnp.float32) + outer, gain_two, shift_two
    )
    return (result, (normed_one, inverse_one, hidden_low, inner, active, normed_two, inverse_two))


def forward(inputs, labels, valid, params):
    query_mat, query_vec, key_mat, value_mat, value_vec = params[0:5]
    token_rows, width = inputs.shape
    head_size = width // HEADS
    scale = head_size ** (-0.5)
    queries = (product(inputs, query_mat) + query_vec).astype(jnp.bfloat16)
    keys = product(inputs, key_mat).astype(jnp.bfloat16)
    values = (product(inputs, value_mat) + value_vec).astype(jnp.bfloat16)
    block_rows = min(512, token_rows)

    def one_block(first_row):
        allowed = labels[:, None] == labels[None, :]

        def one_head(head_index):
            head_queries = lax.dynamic_slice_in_dim(queries, head_index * head_size, head_size, 1)
            head_keys = lax.dynamic_slice_in_dim(keys, head_index * head_size, head_size, 1)
            head_values = lax.dynamic_slice_in_dim(values, head_index * head_size, head_size, 1)
            scores = jnp.where(allowed, product_nt(head_queries, head_keys) * scale, MASKED)
            highest = jnp.max(scores, -1, keepdims=True)
            powers = jnp.exp(scores - highest)
            totals = jnp.sum(powers, -1, keepdims=True)
            shares = (powers / totals).astype(jnp.bfloat16)
            return (product(shares, head_values), (highest + jnp.log(totals))[:, 0])

        head_out, head_lse = lax.map(one_head, jnp.arange(HEADS, dtype=jnp.int32))
        attended = (
            jnp.transpose(head_out, (1, 0, 2)).reshape(block_rows, width).astype(jnp.bfloat16)
        )
        result, unused = tail(inputs, attended, params)
        shown = jnp.where(valid[:, None], result, 0.0).astype(jnp.bfloat16)
        return (attended, head_lse, shown)

    firsts = jnp.arange(token_rows // block_rows, dtype=jnp.int32) * block_rows
    attended, lse_blocks, shown = lax.map(one_block, firsts)
    attended = attended.reshape(token_rows, width)
    shown = shown.reshape(token_rows, width)
    lse_all = jnp.transpose(lse_blocks, (1, 0, 2)).reshape(HEADS, token_rows)
    return ((queries, keys, values, attended, lse_all), shown)


def backward(inputs, labels, cotangent, starts, live, saved, params):
    queries, keys, values, attended, lse_all = saved
    query_mat, key_mat, value_mat, out_mat = (params[0], params[2], params[3], params[5])
    gain_one, inner_mat, outer_mat, gain_two = (params[7], params[9], params[11], params[13])
    token_rows, width = inputs.shape
    head_size = width // HEADS
    scale = head_size ** (-0.5)
    slot_count = starts.shape[0]
    row_inputs = inputs[starts]
    row_attended = attended[starts]
    unused, kept = tail(row_inputs, row_attended, params)
    normed_one, inverse_one, hidden_low, inner, active, normed_two, inverse_two = kept
    upstream = jnp.where(live[:, None], cotangent, 0.0)
    grad_sum_two, grad_gain_two, grad_shift_two = normalize_back(
        upstream, normed_two, inverse_two, gain_two
    )
    grad_outer = grad_sum_two.astype(jnp.bfloat16)
    grad_outer_mat = product_tn(active, grad_outer)
    grad_outer_vec = jnp.sum(grad_outer.astype(jnp.float32), 0)
    grad_inner = (product_nt(grad_outer, outer_mat) * gelu_slope(inner)).astype(jnp.bfloat16)
    grad_inner_mat = product_tn(hidden_low, grad_inner)
    grad_inner_vec = jnp.sum(grad_inner.astype(jnp.float32), 0)
    grad_hidden = grad_sum_two + product_nt(grad_inner, inner_mat)
    grad_sum_one, grad_gain_one, grad_shift_one = normalize_back(
        grad_hidden, normed_one, inverse_one, gain_one
    )
    grad_branch = grad_sum_one.astype(jnp.bfloat16)
    grad_out_mat = product_tn(row_attended, grad_branch)
    grad_out_vec = jnp.sum(grad_branch.astype(jnp.float32), 0)
    grad_attended = (
        product_nt(grad_branch, out_mat).astype(jnp.bfloat16).reshape(slot_count, HEADS, head_size)
    )
    row_queries = queries[starts].reshape(slot_count, HEADS, head_size)
    keys_split = keys.reshape(token_rows, HEADS, head_size)
    values_split = values.reshape(token_rows, HEADS, head_size)
    allowed = labels[starts][None, :, None] == labels[None, None, :]
    scores = (
        jnp.einsum("rhd,thd->hrt", row_queries, keys_split, preferred_element_type=jnp.float32)
        * scale
    )
    shares = jnp.where(allowed, jnp.exp(scores - lse_all[:, starts][:, :, None]), 0.0)
    shares_low = shares.astype(jnp.bfloat16)
    grad_shares = jnp.einsum(
        "rhd,thd->hrt", grad_attended, values_split, preferred_element_type=jnp.float32
    )
    grad_scores = (
        shares * (grad_shares - jnp.sum(grad_shares * shares, -1, keepdims=True))
    ).astype(jnp.bfloat16)
    grad_queries = (
        jnp.einsum("hrt,thd->rhd", grad_scores, keys_split, preferred_element_type=jnp.float32)
        * scale
    )
    grad_queries = grad_queries.reshape(slot_count, width).astype(jnp.bfloat16)
    grad_keys = (
        jnp.einsum("hrt,rhd->thd", grad_scores, row_queries, preferred_element_type=jnp.float32)
        * scale
    )
    grad_keys = grad_keys.reshape(token_rows, width).astype(jnp.bfloat16)
    grad_values = jnp.einsum(
        "hrt,rhd->thd", shares_low, grad_attended, preferred_element_type=jnp.float32
    )
    grad_values = grad_values.reshape(token_rows, width).astype(jnp.bfloat16)
    grad_inputs = product_nt(grad_keys, key_mat) + product_nt(grad_values, value_mat)
    grad_inputs = grad_inputs.at[starts].add(product_nt(grad_queries, query_mat) + grad_sum_one)
    grads = (
        product_tn(row_inputs, grad_queries),
        jnp.sum(grad_queries.astype(jnp.float32), 0),
        product_tn(inputs, grad_keys),
        product_tn(inputs, grad_values),
        jnp.sum(grad_values.astype(jnp.float32), 0),
        grad_out_mat,
        grad_out_vec,
        grad_gain_one,
        grad_shift_one,
        grad_inner_mat,
        grad_inner_vec,
        grad_outer_mat,
        grad_outer_vec,
        grad_gain_two,
        grad_shift_two,
    )
    return (grad_inputs.astype(jnp.bfloat16), grads)


def cast_params(gathered):
    vector_places = (1, 4, 6, 7, 8, 10, 12, 13, 14)
    return tuple(
        (
            item.astype(jnp.float32) if place in vector_places else item
            for place, item in enumerate(gathered)
        )
    )


def split_halves(grads, side):
    keep_list = []
    give_list = []
    for item in grads:
        half = item.shape[0] // 2
        keep_list.append(lax.dynamic_slice_in_dim(item, side * half, half, 0))
        give_list.append(lax.dynamic_slice_in_dim(item, (1 - side) * half, half, 0))
    return (tuple(keep_list), tuple(give_list))


def local(
    hidden_in,
    query_lengths,
    passage_lengths,
    positives,
    query_weight,
    query_bias,
    key_weight,
    value_weight,
    value_bias,
    output_weight,
    output_bias,
    first_gain,
    first_shift,
    inner_weight,
    inner_bias,
    outer_weight,
    outer_bias,
    second_gain,
    second_shift,
):
    stored = (
        query_weight,
        query_bias,
        key_weight,
        value_weight,
        value_bias,
        output_weight,
        output_bias,
        first_gain,
        first_shift,
        inner_weight,
        inner_bias,
        outer_weight,
        outer_bias,
        second_gain,
        second_shift,
    )
    micro = hidden_in.shape[0]
    width = hidden_in.shape[3]
    cls_scale = width ** (-0.5)
    side = lax.axis_index("tower")
    is_query = side == 0
    slot_count = query_lengths.shape[1]
    passage_count = passage_lengths.shape[1]
    half_count = (slot_count + 1) // 2
    extra_rows = 2 * half_count - slot_count
    owners = lax.axis_size(("tower", "batch"))
    totals = tuple(
        (jnp.zeros((item.shape[0] * owners,) + item.shape[1:], jnp.float32) for item in stored)
    )
    half_totals = tuple(
        (jnp.zeros((item.shape[0] * owners // 2,) + item.shape[1:], jnp.float32) for item in stored)
    )
    shown_list = []
    grad_list = []
    for micro_step in range(micro):
        gathered = (
            lax.all_gather(query_weight, ("tower", "batch"), axis=0, tiled=True),
            lax.all_gather(query_bias, ("tower", "batch"), axis=0, tiled=True),
            lax.all_gather(key_weight, ("tower", "batch"), axis=0, tiled=True),
            lax.all_gather(value_weight, ("tower", "batch"), axis=0, tiled=True),
            lax.all_gather(value_bias, ("tower", "batch"), axis=0, tiled=True),
            lax.all_gather(output_weight, ("tower", "batch"), axis=0, tiled=True),
            lax.all_gather(output_bias, ("tower", "batch"), axis=0, tiled=True),
            lax.all_gather(first_gain, ("tower", "batch"), axis=0, tiled=True),
            lax.all_gather(first_shift, ("tower", "batch"), axis=0, tiled=True),
            lax.all_gather(inner_weight, ("tower", "batch"), axis=0, tiled=True),
            lax.all_gather(inner_bias, ("tower", "batch"), axis=0, tiled=True),
            lax.all_gather(outer_weight, ("tower", "batch"), axis=0, tiled=True),
            lax.all_gather(outer_bias, ("tower", "batch"), axis=0, tiled=True),
            lax.all_gather(second_gain, ("tower", "batch"), axis=0, tiled=True),
            lax.all_gather(second_shift, ("tower", "batch"), axis=0, tiled=True),
        )
        params = cast_params(gathered)
        inputs = hidden_in[micro_step, 0]
        passage_part = jnp.pad(passage_lengths[micro_step], (0, slot_count - passage_count))
        lengths = jnp.where(is_query, query_lengths[micro_step], passage_part)
        labels, valid, starts, live = segments(lengths, inputs.shape[0])
        saved, shown = forward(inputs, labels, valid, params)
        shown_list.append(shown)
        mine = jnp.where(live[:, None], shown[starts], 0.0)
        partner = partner_2(mine, "tower", 0)
        query_cls = jnp.where(is_query, mine, partner)
        passage_cls = jnp.where(is_query, partner, mine)[:passage_count]
        pooled = lax.all_gather(passage_cls, "batch", axis=0, tiled=True)
        padded_queries = jnp.pad(query_cls, ((0, extra_rows), (0, 0)))
        padded_targets = jnp.pad(positives[micro_step], (0, extra_rows))
        my_queries = lax.dynamic_slice_in_dim(padded_queries, side * half_count, half_count, 0)
        my_targets = lax.dynamic_slice_in_dim(padded_targets, side * half_count, half_count, 0)
        logits = product_nt(my_queries, pooled) * cls_scale
        highest = jnp.max(logits, -1, keepdims=True)
        powers = jnp.exp(logits - highest)
        shares = powers / jnp.sum(powers, -1, keepdims=True)
        columns = jnp.arange(pooled.shape[0], dtype=jnp.int32)
        target = (columns[None, :] == my_targets[:, None]).astype(jnp.float32)
        grad_logits = ((shares - target) / micro).astype(jnp.bfloat16)
        own_grad = product(grad_logits, pooled) * cls_scale
        pooled_grad = product_tn(grad_logits, my_queries) * cls_scale
        summed = lax.psum_scatter(pooled_grad, "batch", scatter_dimension=0, tiled=True)
        other_queries, other_passages = (
            partner_2(own_grad.astype(jnp.bfloat16), "tower", 0).astype(own_grad.dtype),
            partner_2(summed.astype(jnp.bfloat16), "tower", 0).astype(summed.dtype),
        )
        query_grad = jnp.concatenate([own_grad, other_queries], 0)[:slot_count]
        passage_grad = jnp.pad(summed + other_passages, ((0, slot_count - passage_count), (0, 0)))
        cotangent = jnp.where(is_query, query_grad, passage_grad)
        input_part, step_grads = backward(inputs, labels, cotangent, starts, live, saved, params)
        grad_list.append(input_part)
        totals = tuple((first + second for first, second in zip(totals, step_grads)))
    keep_all, give_all = split_halves(totals, side)
    came_all = jax.tree.map(
        lambda part, own: part.astype(own.dtype), partner_2(as_sent(give_all), "tower", 0), give_all
    )
    half_totals = tuple((first + second for first, second in zip(keep_all, came_all)))
    shards = lax.psum_scatter(half_totals, "batch", scatter_dimension=0, tiled=True)
    hidden_out = jnp.stack(shown_list)[:, None]
    input_grad = jnp.stack(grad_list)[:, None]
    return (
        hidden_out,
        input_grad,
        shards[0],
        shards[1],
        shards[2],
        shards[3],
        shards[4],
        shards[5],
        shards[6],
        shards[7],
        shards[8],
        shards[9],
        shards[10],
        shards[11],
        shards[12],
        shards[13],
        shards[14],
    )


def solution(mesh):
    placed = (
        P(None, "tower", "batch", None),
        P(None, "batch"),
        P(None, "batch"),
        P(None, "batch"),
        P(("tower", "batch"), None),
        P(("tower", "batch")),
        P(("tower", "batch"), None),
        P(("tower", "batch"), None),
        P(("tower", "batch")),
        P(("tower", "batch"), None),
        P(("tower", "batch")),
        P(("tower", "batch")),
        P(("tower", "batch")),
        P(("tower", "batch"), None),
        P(("tower", "batch")),
        P(("tower", "batch"), None),
        P(("tower", "batch")),
        P(("tower", "batch")),
        P(("tower", "batch")),
    )
    return jax.shard_map(
        local,
        mesh=mesh,
        in_specs=placed,
        out_specs=(
            P(None, "tower", "batch", None),
            P(None, "tower", "batch", None),
            P(("tower", "batch"), None),
            P(("tower", "batch")),
            P(("tower", "batch"), None),
            P(("tower", "batch"), None),
            P(("tower", "batch")),
            P(("tower", "batch"), None),
            P(("tower", "batch")),
            P(("tower", "batch")),
            P(("tower", "batch")),
            P(("tower", "batch"), None),
            P(("tower", "batch")),
            P(("tower", "batch"), None),
            P(("tower", "batch")),
            P(("tower", "batch")),
            P(("tower", "batch")),
        ),
        check_vma=False,
    )
```

profile of v0, /device:TPU:0, one launch (start us, length us, event | category | flops | bytes accessed | tf_op | source)
XLA Modules:
  0.0 1010.5 jit_solution(10408570091418277929)
XLA Ops:
  24.5 42.5 %all-reduce.30 = (bf16[3072]{0:T(1024)(128)(2,1)S(1)}, bf16[768]{0:T(1024)(128)(2,1)S(1)}, bf16[768]{0:T(1024)(128)(2,1)S(1)}, bf16[768]{0:T(1024)(128)(2,1)S(1)...) all-reduce(bf16[3072]{0:T(1024)(128)(2,1)S(1)} %dynamic-update-slic, ...), channel_id=1, replica_groups=mesh['tower'=2,'batch'=16] {'tower','batch'}, use_global_device_ids=true, to_apply=%add.13 | all-reduce | flops 9216 | bytes 36864
  82.3 41.5 %all-gather.13.cloned.1.call-done = bf16[768,768]{1,0:T(8,128)(2,1)} async-done(((bf16[24,768]{1,0:T(8,128)(2,1)}), bf16[768,768]{1,0:T(8,128)(2,1)}) %all-gather.13.cloned.1.call-update) | async-done | bytes 1179664 | tf_op jit(solution)/shard_map/all_gather | solution.py:288
  126.8 53.0 %all-gather.9.cloned.1.call-done = bf16[768,768]{1,0:T(8,128)(2,1)} async-done(((bf16[24,768]{1,0:T(8,128)(2,1)}), bf16[768,768]{1,0:T(8,128)(2,1)}) %all-gather.9.cloned.1.call-update) | async-done | bytes 1179664 | tf_op jit(solution)/shard_map/all_gather | solution.py:285
  179.8 2.9 add_convert_fusion.5
  183.9 72.9 %while.46 = (s32[]{:T(128)}, bf16[12,512,64]{1,2,0:T(8,128)(2,1)S(1)}, f32[12,512]{1,0:T(8,128)}, s32[12]{0:T(128)}, bf16[512,768]{1,0:T(8,128)(2,1)}, /*index=5...) while((s32[]{:T(128)}, ...), condition=%wide.region_5.6_spmd.clone, body=%wide.region_2.5_spmd.clone.sunk | while | flops 69467648 | bytes 3695811 | solution.py:107
  262.8 50.3 %while.47 = (s32[]{:T(128)}, bf16[12,512,64]{1,2,0:T(8,128)(2,1)S(1)}, f32[12,512]{1,0:T(8,128)S(1)}, s32[12]{0:T(128)S(1)}, bf16[512,768]{1,0:T(8,128)(2,1)}, /...) while((s32[]{:T(128)}, ...), condition=%wide.region_15.16_spmd.clone, body=%wide.region_12.15_spmd.clone.sunk | while | flops 69467648 | bytes 3695811 | solution.py:107
  351.5 14.6 %all-gather.19.cloned.1.call-done = bf16[3072,768]{1,0:T(8,128)(2,1)} async-done(((bf16[96,768]{1,0:T(8,128)(2,1)}), bf16[3072,768]{1,0:T(8,128)(2,1)}) %all-gather.19.cloned.1.call-update) | async-done | bytes 4718608 | tf_op jit(solution)/shard_map/all_gather | solution.py:296
  366.1 21.9 %fusion.217 = (f32[512]{0:T(512)S(1)}, f32[512,768]{1,0:T(8,128)S(1)}) fusion(f32[768]{0:T(1024)S(1)} %copy-done.119, bf16[3072,768]{1,0:T(8,128)(2,1)} %all-gather.19.cloned.1.call-done, bf16[768,3072]{1,0:T(8,128)(2,1)} %all-gather.17.cloned.1.call-done, f32[3072]{0:T(1024)S(1)} %copy-done.77, f32[512,768]{1,0:T(8,128)} %copy-done.45, ...), kind=kOutput, calls=%fused_computation.461 | convolution fusion | flops 4941151744 | bytes 12610560 | tf_op jit(solution)/shard_map/while/body/eval_jaxpr/dot_general | solution.py:22
  388.0 22.3 %fusion.215 = (f32[512]{0:T(512)S(1)}, f32[512,768]{1,0:T(8,128)S(1)}) fusion(f32[768]{0:T(1024)S(1)} %copy-done.119, bf16[3072,768]{1,0:T(8,128)(2,1)} %all-gather.19.cloned.1.call-done, bf16[768,3072]{1,0:T(8,128)(2,1)} %all-gather.17.cloned.1.call-done, f32[3072]{0:T(1024)S(1)} %copy-done.77, f32[512,768]{1,0:T(8,128)} %copy-done.44, ...), kind=kOutput, calls=%fused_computation.459 | convolution fusion | flops 4941151744 | bytes 12610560 | tf_op jit(solution)/shard_map/while/body/eval_jaxpr/dot_general | solution.py:22
  419.1 3.2 convolution_add_fusion.3
  427.5 20.3 %all-gather.1 = bf16[16,2,768]{2,1,0:T(2,128)(2,1)S(1)} all-gather(bf16[1,2,768]{2,1,0:T(2,128)(2,1)S(1)} %fusion.129), channel_id=1, replica_groups=mesh['tower'=2,'batch'=16] {'batch'}, dimensions={0}, use_global_device_ids=true | all-gather | bytes 52224 | tf_op jit(solution)/shard_map/all_gather | solution.py:312
  449.4 17.6 %all-gather = bf16[16,2,768]{2,1,0:T(2,128)(2,1)S(1)} all-gather(bf16[1,2,768]{2,1,0:T(2,128)(2,1)S(1)} %fusion.128), channel_id=1, replica_groups=mesh['tower'=2,'batch'=16] {'batch'}, dimensions={0}, use_global_device_ids=true | all-gather | bytes 52224 | tf_op jit(solution)/shard_map/all_gather | solution.py:312
  473.1 85.2 %all-reduce.33.cloned.1.call-done = (f32[32,768]{1,0:T(8,128)}, f32[32,768]{1,0:T(8,128)}) async-done(((f32[32,768]{1,0:T(8,128)}, f32[32,768]{1,0:T(8,128)}), (f32[32,768]{1,0:T(8,128)}, f32[32,768]{1,0:T(8,128)})) %all-reduce.33.cloned.1.call-update) | async-done | bytes 196624
  566.0 4.4 convert_reduce_fusion.3
  570.5 4.4 multiply_reduce_fusion.9
  594.9 8.6 collective-permute-done.9
  615.2 7.8 collective-permute-done.8
  630.6 5.7 convolution_add_fusion
  646.2 57.7 %collective-permute-done.6 = bf16[384,768]{1,0:T(8,128)(2,1)S(1)} collective-permute-done((bf16[384,768]{1,0:T(8,128)(2,1)S(1)}, bf16[384,768]{1,0:T(8,128)(2,1)S(1)}, u32[]{:S(2)}, u32[]{:S(2)}) %collective-permute-start.6) | collective-permute-done | bytes 589856 | tf_op jit(solution)/shard_map/ppermute | solution.py:14
  705.1 5.7 convert_add_fusion
  716.2 46.3 %collective-permute-done.15 = bf16[384,3072]{1,0:T(8,128)(2,1)S(1)} collective-permute-done((bf16[384,3072]{1,0:T(8,128)(2,1)S(1)}, bf16[384,3072]{1,0:T(8,128)(2,1)S(1)}, u32[]{:S(2)}, u32[]{:S(2)}) %collective-permute-start.15) | collective-permute-done | bytes 2359328 | tf_op jit(solution)/shard_map/ppermute | solution.py:14
  798.3 58.0 %all-reduce.28 = (f32[384]{0:T(512)S(1)}, f32[384]{0:T(512)S(1)}, f32[384]{0:T(512)S(1)}, f32[384]{0:T(512)S(1)}, f32[384]{0:T(512)S(1)}, /*index=5*/f32[1536]{0...) all-reduce(f32[384]{0:T(512)S(1)} %convert_add_fusion.14, ...), channel_id=5, replica_groups=mesh['tower'=2,'batch'=16] {'batch'}, use_global_device_ids=true, to_apply=%region_49.50.clone | all-reduce | flops 4608 | bytes 36864
  861.6 62.7 %reduce-scatter.17.cloned.1.call-done = f32[96,768]{1,0:T(8,128)} async-done(((f32[1536,768]{1,0:T(8,128)}), f32[96,768]{1,0:T(8,128)}) %reduce-scatter.17.cloned.1.call-update) | async-done | bytes 294928 | tf_op jit(solution)/shard_map/reduce_scatter | solution.py:342
  924.2 79.6 %reduce-scatter.15.cloned.1.call-done = f32[24,3072]{1,0:T(8,128)} async-done(((f32[384,3072]{1,0:T(8,128)}), f32[24,3072]{1,0:T(8,128)}) %reduce-scatter.15.cloned.1.call-update) | async-done | bytes 294928 | tf_op jit(solution)/shard_map/reduce_scatter | solution.py:342
  (746 shorter events, 309.9 us)
Async XLA Ops:
  7.2 72.2 %all-gather.11.cloned.1.call-start = ((), (), s32[]{:S(2)}) async-start(), calls=%async_computation.7 | async-start | bytes 1216512 | tf_op jit(solution)/shard_map/all_gather | solution.py:287
  7.9 115.9 %all-gather.13.cloned.1.call-start = ((), (), s32[]{:S(2)}) async-start(), calls=%async_computation.8 | async-start | bytes 1216512 | tf_op jit(solution)/shard_map/all_gather | solution.py:288
  8.7 171.1 %all-gather.9.cloned.1.call-start = ((), (), s32[]{:S(2)}) async-start(), calls=%async_computation.6 | async-start | bytes 1216512 | tf_op jit(solution)/shard_map/all_gather | solution.py:285
  9.4 331.8 %all-gather.15.cloned.1.call-start = ((), (), s32[]{:S(2)}) async-start(), calls=%async_computation.9 | async-start | bytes 1216512 | tf_op jit(solution)/shard_map/all_gather | solution.py:290
  10.0 341.5 %all-gather.17.cloned.1.call-start = ((), (), s32[]{:S(2)}) async-start(), calls=%async_computation.10 | async-start | bytes 4866048 | tf_op jit(solution)/shard_map/all_gather | solution.py:294
  10.6 355.5 %all-gather.19.cloned.1.call-start = ((), (), s32[]{:S(2)}) async-start(), calls=%async_computation.11 | async-start | bytes 4866048 | tf_op jit(solution)/shard_map/all_gather | solution.py:296
  11.2 547.1 %all-reduce.33.cloned.1.call-start = ((), (), s32[]{:S(2)}) async-start(), calls=%async_computation.18 | async-start | bytes 393216
  418.5 31.0 %collective-permute-start = (bf16[17,768]{1,0:T(8,128)(2,1)S(1)}, bf16[17,768]{1,0:T(8,128)(2,1)S(1)}, u32[]{:S(2)}, u32[]{:S(2)}) collective-permute-start(bf16[17,768]{1,0:T(8,128)(2,1)S(1)} %broadcast_select_fusion.1), channel_id=1, source_target_pairs={{0,16},{16,0},{1,17},{17,1},{2,18},{18,2},{3,19},{19,3},{4,20},{20... | collective-permute-start | bytes 78344 | tf_op jit(solution)/shard_map/ppermute | solution.py:14
  470.7 390.8 %reduce-scatter.21.cloned.1.call-start = ((), (), s32[]{:S(2)}) async-start(), calls=%async_computation.17 | async-start | bytes 1253376
  590.4 13.0 %collective-permute-start.9 = (bf16[384,768]{0,1:T(8,128)(2,1)S(1)}, bf16[384,768]{0,1:T(8,128)(2,1)S(1)}, u32[]{:S(2)}, u32[]{:S(2)}) collective-permute-start(bf16[384,768]{0,1:T(8,128)(2,1)S(1)} %fusion.77), channel_id=1, source_target_pairs={{0,16},{16,0},{1,17},{17,1},{2,18},{18,2},{3,19},{19,3},{4,20},{20... | collective-permute-start | bytes 1769480 | tf_op jit(solution)/shard_map/ppermute | solution.py:14
  605.1 256.5 %reduce-scatter.19.cloned.1.call-start = ((), (), s32[]{:S(2)}) async-start(), calls=%async_computation.16 | async-start | bytes 1253376
  610.7 12.4 %collective-permute-start.8 = (bf16[384,768]{0,1:T(8,128)(2,1)}, bf16[384,768]{0,1:T(8,128)(2,1)}, u32[]{:S(2)}, u32[]{:S(2)}) collective-permute-start(bf16[384,768]{0,1:T(8,128)(2,1)} %fusion.76), channel_id=1, source_target_pairs={{0,16},{16,0},{1,17},{17,1},{2,18},{18,2},{3,19},{19,3},{4,20},{20... | collective-permute-start | bytes 1769480 | tf_op jit(solution)/shard_map/ppermute | solution.py:14
  626.1 235.5 %reduce-scatter.13.cloned.1.call-start = ((), (), s32[]{:S(2)}) async-start(), calls=%async_computation.13 | async-start | bytes 1253376 | tf_op jit(solution)/shard_map/reduce_scatter | solution.py:342
  640.2 221.3 %reduce-scatter.11.cloned.1.call-start = ((), (), s32[]{:S(2)}) async-start(), calls=%async_computation.12 | async-start | bytes 1253376 | tf_op jit(solution)/shard_map/reduce_scatter | solution.py:342
  642.9 62.2 %collective-permute-start.17 = (bf16[1536,768]{1,0:T(8,128)(2,1)S(1)}, bf16[1536,768]{1,0:T(8,128)(2,1)}, u32[]{:S(2)}, u32[]{:S(2)}) collective-permute-start(bf16[1536,768]{1,0:T(8,128)(2,1)S(1)} %dynamic-slice_convert_fusion), channel_id=1, source_target_pairs={{0,16},{16,0},{1,17},{17,1},{2,18},{18,2},{3,19},{19,3},{4,20},{20... | collective-permute-start | bytes 7077896 | tf_op jit(solution)/shard_map/ppermute | solution.py:14
  645.1 58.8 %collective-permute-start.6 = (bf16[384,768]{1,0:T(8,128)(2,1)S(1)}, bf16[384,768]{1,0:T(8,128)(2,1)S(1)}, u32[]{:S(2)}, u32[]{:S(2)}) collective-permute-start(bf16[384,768]{1,0:T(8,128)(2,1)S(1)} %dynamic-slice_convert_fusion.5), channel_id=1, source_target_pairs={{0,16},{16,0},{1,17},{17,1},{2,18},{18,2},{3,19},{19,3},{4,20},{20... | collective-permute-start | bytes 1769480 | tf_op jit(solution)/shard_map/ppermute | solution.py:14
  705.1 219.2 %reduce-scatter.17.cloned.1.call-start = ((), (), s32[]{:S(2)}) async-start(), calls=%async_computation.15 | async-start | bytes 5013504 | tf_op jit(solution)/shard_map/reduce_scatter | solution.py:342
  710.9 292.9 %reduce-scatter.15.cloned.1.call-start = ((), (), s32[]{:S(2)}) async-start(), calls=%async_computation.14 | async-start | bytes 5013504 | tf_op jit(solution)/shard_map/reduce_scatter | solution.py:342
  715.0 47.5 %collective-permute-start.15 = (bf16[384,3072]{1,0:T(8,128)(2,1)S(1)}, bf16[384,3072]{1,0:T(8,128)(2,1)S(1)}, u32[]{:S(2)}, u32[]{:S(2)}) collective-permute-start(bf16[384,3072]{1,0:T(8,128)(2,1)S(1)} %dynamic-slice_convert_fusion.1), channel_id=1, source_target_pairs={{0,16},{16,0},{1,17},{17,1},{2,18},{18,2},{3,19},{19,3},{4,20},{20... | collective-permute-start | bytes 7077896 | tf_op jit(solution)/shard_map/ppermute | solution.py:14
  770.2 18.8 %collective-permute-start.19 = (bf16[384]{0:T(512)(128)(2,1)}, bf16[384]{0:T(512)(128)(2,1)}, u32[]{:S(2)}, u32[]{:S(2)}) collective-permute-start(bf16[384]{0:T(512)(128)(2,1)} %dynamic_slice.223), channel_id=1, source_target_pairs={{0,16},{16,0},{1,17},{17,1},{2,18},{18,2},{3,19},{19,3},{4,20},{20... | collective-permute-start | bytes 2312 | tf_op jit(solution)/shard_map/ppermute | solution.py:14
  771.4 19.1 %collective-permute-start.20 = (bf16[384]{0:T(512)(128)(2,1)}, bf16[384]{0:T(512)(128)(2,1)}, u32[]{:S(2)}, u32[]{:S(2)}) collective-permute-start(bf16[384]{0:T(512)(128)(2,1)} %dynamic_slice.222), channel_id=1, source_target_pairs={{0,16},{16,0},{1,17},{17,1},{2,18},{18,2},{3,19},{19,3},{4,20},{20... | collective-permute-start | bytes 2312 | tf_op jit(solution)/shard_map/ppermute | solution.py:14
  772.2 20.2 %collective-permute-start.18 = (bf16[384]{0:T(512)(128)(2,1)}, bf16[384]{0:T(512)(128)(2,1)}, u32[]{:S(2)}, u32[]{:S(2)}) collective-permute-start(bf16[384]{0:T(512)(128)(2,1)} %dynamic_slice.224), channel_id=1, source_target_pairs={{0,16},{16,0},{1,17},{17,1},{2,18},{18,2},{3,19},{19,3},{4,20},{20... | collective-permute-start | bytes 2312 | tf_op jit(solution)/shard_map/ppermute | solution.py:14
  774.8 22.7 %collective-permute-start.16 = (bf16[1536]{0:T(1024)(128)(2,1)}, bf16[1536]{0:T(1024)(128)(2,1)}, u32[]{:S(2)}, u32[]{:S(2)}) collective-permute-start(bf16[1536]{0:T(1024)(128)(2,1)} %dynamic_slice.221), channel_id=1, source_target_pairs={{0,16},{16,0},{1,17},{17,1},{2,18},{18,2},{3,19},{19,3},{4,20},{20... | collective-permute-start | bytes 9224 | tf_op jit(solution)/shard_map/ppermute | solution.py:14
  776.3 17.7 %collective-permute-start.13 = (bf16[384]{0:T(512)(128)(2,1)}, bf16[384]{0:T(512)(128)(2,1)}, u32[]{:S(2)}, u32[]{:S(2)}) collective-permute-start(bf16[384]{0:T(512)(128)(2,1)} %dynamic_slice.226), channel_id=1, source_target_pairs={{0,16},{16,0},{1,17},{17,1},{2,18},{18,2},{3,19},{19,3},{4,20},{20... | collective-permute-start | bytes 2312 | tf_op jit(solution)/shard_map/ppermute | solution.py:14
  (150 other events, 2531.6 us)
Sparse Core Ops, SparseCore 0:
  10.9 56.9 all-gather.10
  70.8 52.9 all-gather.12
  126.8 52.9 all-gather.8
  182.6 53.0 all-gather.14
  238.4 62.4 all-gather.16
  303.6 62.4 all-gather.18
  470.8 87.3 all-reduce.32
  605.2 56.2 reduce-scatter.20
  665.7 56.9 reduce-scatter.18
  726.8 57.0 reduce-scatter.12
  788.1 57.2 reduce-scatter.10
  849.7 74.5 reduce-scatter.16
  929.2 74.6 reduce-scatter.14
where the time goes:
time: 1020 us; the launch traced here: 1010 us
  waiting for transfers between devices  468 us (46%)
  matrix products  186 us (18%)
  blocking collectives  138 us (14%)
  local copies, waits for them, and re-layouts  114 us (11%)
  other arithmetic  46.6 us (5%)
  starting transfers between devices  22.1 us (2%)
  between operations  18.2 us (2%)
  loops' own time  16.6 us (2%)
    reduce_scatter x4, waiting for transfers between devices, local(): lax.psum_scatter(half_totals, 'batch', scatter_dimension=0, tiled=True)  142 us
    ppermute x21, waiting for transfers between devices, partner_2(): lax.ppermute(x, axis, [(i, i ^ 1 << apart) for i in range(lax.axis_size(a...  128 us
    dot_general x42, matrix products, product(): return jnp.dot(left, right, preferred_element_type=jnp.float32)  101 us
    unnamed x2, blocking collectives  100 us
    unnamed x16, waiting for transfers between devices  88.9 us
    dot_general x38, matrix products, product_nt(): jnp.einsum('ra,ba->rb', left, right, preferred_element_type=jnp.float32)  53.1 us
    all_gather x1, waiting for transfers between devices, local(): lax.all_gather(query_weight, ('tower', 'batch'), axis=0, tiled=True)  53 us
    all_gather x1, waiting for transfers between devices, local(): lax.all_gather(value_weight, ('tower', 'batch'), axis=0, tiled=True)  41.5 us
  transfers between devices with their start and end apart: 34, of which 16 were waited for; matrix products, arithmetic and copies ran while one was open for 26% of the time, Pallas kernels for 0%

commit v1 on v0

--- a/solution.py
+++ b/solution.py
@@ -1,6 +1,10 @@
+import functools
+
 import jax
 import jax.numpy as jnp
 from jax import lax
+from jax.experimental import pallas as pl
+from jax.experimental.pallas import tpu as pltpu
 from jax.sharding import PartitionSpec as P
 
 HEADS = 12
@@ -222,6 +226,570 @@
         keep_list.append(lax.dynamic_slice_in_dim(item, side * half, half, 0))
         give_list.append(lax.dynamic_slice_in_dim(item, (1 - side) * half, half, 0))
     return (tuple(keep_list), tuple(give_list))
+
+
+MESH = pl.DeviceIdType.MESH
+BLOCK = 40
+
+
+class Place:
+    def __init__(self):
+        self.x = lax.axis_index("tower")
+        batch = lax.axis_index("batch")
+        self.core = batch % 2
+        self.y = (batch // 2) % 2
+        self.z = batch // 4
+
+    def device(self, x=None, y=None, z=None, core=None):
+        x = self.x if x is None else x
+        y = self.y if y is None else y
+        z = self.z if z is None else z
+        core = self.core if core is None else core
+        return (x, z * 4 + y * 2 + core)
+
+    def chip(self, x=None, y=None, z=None):
+        x = self.x if x is None else x
+        y = self.y if y is None else y
+        z = self.z if z is None else z
+        return x * 8 + z * 2 + y
+
+    def layer(self, step):
+        if step == 0:
+            return self.z
+        if step == 1:
+            return self.z + 1 - 2 * (self.z % 2)
+        if step == 2:
+            return (self.z + 2) % 4
+        return 3 - self.z
+
+
+def greet(place):
+    barrier = pltpu.get_barrier_semaphore()
+    peers = [place.device(z=place.layer(step)) for step in (1, 2, 3)]
+    peers += [place.device(x=1 - place.x), place.device(y=1 - place.y), place.device(core=1 - place.core)]
+    for peer in peers:
+        pl.semaphore_signal(barrier, inc=1, device_id=peer, device_id_type=MESH)
+    pl.semaphore_wait(barrier, len(peers))
+
+
+class Sender:
+    def __init__(self, send_sems, recv_sems):
+        self.send_sems = send_sems
+        self.recv_sems = recv_sems
+        self.used = 0
+        self.open = []
+
+    def send(self, src, dst, slot, peer):
+        copy = pltpu.make_async_remote_copy(
+            src_ref=src,
+            dst_ref=dst,
+            send_sem=self.send_sems.at[self.used],
+            recv_sem=self.recv_sems.at[slot],
+            device_id=peer,
+            device_id_type=MESH,
+        )
+        self.used += 1
+        copy.start()
+        self.open.append(copy)
+
+    def arrived(self, dst, slot, peer):
+        pltpu.make_async_remote_copy(
+            src_ref=dst,
+            dst_ref=dst,
+            send_sem=self.send_sems.at[0],
+            recv_sem=self.recv_sems.at[slot],
+            device_id=peer,
+            device_id_type=MESH,
+        ).wait_recv()
+
+    def close(self):
+        for copy in self.open:
+            copy.wait_send()
+        self.open = []
+
+
+def slot_of(chunk, kind, place_index):
+    return (chunk * 9 + kind) * 4 + place_index
+
+
+def gather_kernel(widths, wide_ref, tall_ref, all_wide, all_tall, stage, send_sems, recv_sems):
+    place = Place()
+    sender = Sender(send_sems, recv_sems)
+    greet(place)
+    own_rows = wide_ref.shape[0] * 3 // 4
+    tall_rows = tall_ref.shape[0]
+    sibling = place.device(core=1 - place.core)
+    starts = [0, 2 * widths[0]]
+    offsets = [0, widths[0]]
+
+    def wide_view(ref, chunk, core, chip):
+        rows = pl.ds(pl.multiple_of(chip * 2 * own_rows, 16), 2 * own_rows)
+        first = pl.multiple_of(starts[chunk] + core * widths[chunk], 128)
+        return ref.at[rows, pl.ds(first, widths[chunk])]
+
+    def view(chunk, core, chip):
+        if chunk < 2:
+            return wide_view(all_wide, chunk, core, chip)
+        rows = pl.ds(pl.multiple_of((chip * 2 + core) * tall_rows, 16), tall_rows)
+        return all_tall.at[rows, :]
+
+    for chunk in range(2):
+        first = pl.multiple_of(starts[chunk] + (1 - place.core) * widths[chunk], 128)
+        sender.send(
+            wide_ref.at[:, pl.ds(first, widths[chunk])],
+            stage.at[:, pl.ds(offsets[chunk], widths[chunk])],
+            slot_of(chunk, 8, 0),
+            sibling,
+        )
+    own_tall = view(2, place.core, place.chip())
+    own_tall[...] = tall_ref[...]
+
+    def assemble(chunk):
+        landed = stage.at[:, pl.ds(offsets[chunk], widths[chunk])]
+        sender.arrived(landed, slot_of(chunk, 8, 0), sibling)
+        first = pl.multiple_of(starts[chunk] + place.core * widths[chunk], 128)
+        mine = wide_ref[pl.ds(0, own_rows), pl.ds(first, widths[chunk])].astype(jnp.float32)
+        other = stage[pl.ds(0, own_rows), pl.ds(offsets[chunk], widths[chunk])].astype(jnp.float32)
+        is_first = place.core == 0
+        joined = jnp.concatenate([jnp.where(is_first, mine, other), jnp.where(is_first, other, mine)], 0)
+        rows = pl.ds(pl.multiple_of(place.chip() * 2 * own_rows, 16), 2 * own_rows)
+        all_wide[rows, pl.ds(first, widths[chunk])] = joined.astype(jnp.bfloat16)
+
+    def begin(chunk):
+        own = view(chunk, place.core, place.chip())
+        for step in (3, 2, 1):
+            sender.send(own, own, slot_of(chunk, 0, place.z), place.device(z=place.layer(step)))
+        sender.send(own, own, slot_of(chunk, 1, place.z), place.device(x=1 - place.x))
+        sender.send(own, own, slot_of(chunk, 2, place.z), place.device(y=1 - place.y))
+        sender.send(own, own, slot_of(chunk, 4, place.z), sibling)
+
+    def along(chunk):
+        for step in (1, 2, 3):
+            layer = place.layer(step)
+            block = view(chunk, place.core, place.chip(z=layer))
+            sender.arrived(block, slot_of(chunk, 0, layer), sibling)
+            sender.send(block, block, slot_of(chunk, 1, layer), place.device(x=1 - place.x))
+            sender.send(block, block, slot_of(chunk, 2, layer), place.device(y=1 - place.y))
+            sender.send(block, block, slot_of(chunk, 4, layer), sibling)
+
+    def across(chunk):
+        for step in range(4):
+            layer = place.layer(step)
+            from_x = view(chunk, place.core, place.chip(x=1 - place.x, z=layer))
+            sender.arrived(from_x, slot_of(chunk, 1, layer), sibling)
+            if step < 2:
+                sender.send(from_x, from_x, slot_of(chunk, 3, layer), place.device(y=1 - place.y))
+            sender.send(from_x, from_x, slot_of(chunk, 5, layer), sibling)
+            from_y = view(chunk, place.core, place.chip(y=1 - place.y, z=layer))
+            sender.arrived(from_y, slot_of(chunk, 2, layer), sibling)
+            if step >= 2:
+                sender.send(from_y, from_y, slot_of(chunk, 3, layer), place.device(x=1 - place.x))
+            sender.send(from_y, from_y, slot_of(chunk, 6, layer), sibling)
+
+    def corner(chunk):
+        for step in range(4):
+            layer = place.layer(step)
+            block = view(chunk, place.core, place.chip(x=1 - place.x, y=1 - place.y, z=layer))
+            sender.arrived(block, slot_of(chunk, 3, layer), sibling)
+            sender.send(block, block, slot_of(chunk, 7, layer), sibling)
+
+    def twin(chunk):
+        for step in range(4):
+            layer = place.layer(step)
+            for kind, x, y in ((4, 0, 0), (5, 1, 0), (6, 0, 1), (7, 1, 1)):
+                chip = place.chip(
+                    x=1 - place.x if x else place.x, y=1 - place.y if y else place.y, z=layer
+                )
+                sender.arrived(view(chunk, 1 - place.core, chip), slot_of(chunk, kind, layer), sibling)
+
+    assemble(0)
+    begin(0)
+    assemble(1)
+    begin(1)
+    begin(2)
+    for chunk in range(3):
+        along(chunk)
+        across(chunk)
+        corner(chunk)
+    for chunk in range(3):
+        twin(chunk)
+    sender.close()
+
+
+def gather_weights(wide, tall, widths):
+    owners = lax.axis_size(("tower", "batch"))
+    rows = wide.shape[0] * 3 // 4
+    return pl.pallas_call(
+        functools.partial(gather_kernel, widths),
+        out_shape=(
+            jax.ShapeDtypeStruct((rows * owners, wide.shape[1]), wide.dtype),
+            jax.ShapeDtypeStruct((tall.shape[0] * owners, tall.shape[1]), tall.dtype),
+        ),
+        in_specs=[pl.BlockSpec(memory_space=pltpu.VMEM)] * 2,
+        out_specs=[pl.BlockSpec(memory_space=pltpu.VMEM)] * 2,
+        scratch_shapes=[
+            pltpu.VMEM((wide.shape[0], wide.shape[1] // 2), wide.dtype),
+            pltpu.SemaphoreType.DMA((100,)),
+            pltpu.SemaphoreType.DMA((108,)),
+        ],
+        compiler_params=pltpu.CompilerParams(
+            collective_id=0, has_side_effects=True, vmem_limit_bytes=48 * 2**20
+        ),
+    )(wide, tall)
+
+
+def cls_kernel(block_ref, out_ref, merged, stage, send_sems, recv_sems):
+    place = Place()
+    sender = Sender(send_sems, recv_sems)
+    greet(place)
+    rows, width = block_ref.shape
+    half = width // 2
+    sibling = place.device(core=1 - place.core)
+    across_x = place.device(x=1 - place.x)
+    mine = pl.ds(pl.multiple_of(place.core * half, 128), half)
+    other = pl.ds(pl.multiple_of((1 - place.core) * half, 128), half)
+    sender.send(block_ref.at[:, other], stage.at[0], 0, sibling)
+    sender.arrived(stage.at[0], 0, sibling)
+    merged[...] = (block_ref[:, mine].astype(jnp.float32) + stage[0].astype(jnp.float32)).astype(jnp.bfloat16)
+    sender.send(merged, stage.at[1], 1, across_x)
+    sender.arrived(stage.at[1], 1, across_x)
+
+    def view(core, y, z):
+        first = pl.multiple_of((z * 2 + y) * rows, 16)
+        return out_ref.at[pl.ds(first, rows), pl.ds(pl.multiple_of(core * half, 128), half)]
+
+    own = view(place.core, place.y, place.z)
+    own[...] = (merged[...].astype(jnp.float32) + stage[1].astype(jnp.float32)).astype(jnp.bfloat16)
+    for step in (3, 2, 1):
+        sender.send(own, own, 2 + place.z, place.device(z=place.layer(step)))
+    for step in range(4):
+        layer = place.layer(step)
+        block = view(place.core, place.y, layer)
+        if step > 0:
+            sender.arrived(block, 2 + layer, sibling)
+        sender.send(block, block, 6 + layer, place.device(y=1 - place.y))
+        sender.send(block, block, 10 + layer, sibling)
+    for step in range(4):
+        layer = place.layer(step)
+        block = view(place.core, 1 - place.y, layer)
+        sender.arrived(block, 6 + layer, sibling)
+        sender.send(block, block, 14 + layer, sibling)
+    for step in range(4):
+        layer = place.layer(step)
+        sender.arrived(view(1 - place.core, place.y, layer), 10 + layer, sibling)
+        sender.arrived(view(1 - place.core, 1 - place.y, layer), 14 + layer, sibling)
+    sender.close()
+
+
+def gather_cls(block):
+    rows, width = block.shape
+    chips = lax.axis_size("batch") // 2
+    return pl.pallas_call(
+        cls_kernel,
+        out_shape=jax.ShapeDtypeStruct((rows * chips, width), block.dtype),
+        in_specs=[pl.BlockSpec(memory_space=pltpu.VMEM)],
+        out_specs=pl.BlockSpec(memory_space=pltpu.VMEM),
+        scratch_shapes=[
+            pltpu.VMEM((rows, width // 2), block.dtype),
+            pltpu.VMEM((2, rows, width // 2), block.dtype),
+            pltpu.SemaphoreType.DMA((20,)),
+            pltpu.SemaphoreType.DMA((18,)),
+        ],
+        compiler_params=pltpu.CompilerParams(
+            collective_id=1, has_side_effects=True, vmem_limit_bytes=48 * 2**20
+        ),
+    )(block)
+
+
+def scatter_kernel(part_ref, out_ref, work, stage_core, stage_pair, stage_z, final, stage_last, send_sems, recv_sems):
+    place = Place()
+    sender = Sender(send_sems, recv_sems)
+    greet(place)
+    half = part_ref.shape[1] // 2
+    chip_rows = part_ref.shape[0] // 16
+    sibling = place.device(core=1 - place.core)
+    mine = pl.ds(pl.multiple_of(place.core * half, 128), half)
+    other = pl.ds(pl.multiple_of((1 - place.core) * half, 128), half)
+    other_x, other_y = place.device(x=1 - place.x), place.device(y=1 - place.y)
+
+    def rows_of(x, y, z):
+        return pl.ds(pl.multiple_of(place.chip(x, y, z) * chip_rows, 16), chip_rows)
+
+    flips = [(1, 1), (1, 0), (0, 1), (0, 0)]
+    blocks = [(dx, dy, z) for z in range(4) for dx, dy in flips]
+
+    def target(dx, dy):
+        return (1 - place.x if dx else place.x, 1 - place.y if dy else place.y)
+
+    def rows_for(dx, dy, z):
+        x, y = target(dx, dy)
+        return rows_of(x, y, z)
+
+    def first_dim(z):
+        return 0 if z % 2 == 0 else 1
+
+    for index, (dx, dy, z) in enumerate(blocks):
+        rows = rows_for(dx, dy, z)
+        sender.send(part_ref.at[rows, other], stage_core.at[index], index, sibling)
+    base = 16
+    for index, (dx, dy, z) in enumerate(blocks):
+        sender.arrived(stage_core.at[index], index, sibling)
+        rows = rows_for(dx, dy, z)
+        total = part_ref[rows, mine].astype(jnp.float32) + stage_core[index].astype(jnp.float32)
+        work[index] = total.astype(jnp.bfloat16)
+        goes_first = dx if first_dim(z) == 0 else dy
+        if goes_first:
+            peer = other_x if first_dim(z) == 0 else other_y
+            sender.send(work.at[index], stage_pair.at[index], base + index, peer)
+    base_second = 32
+    for z in range(4):
+        dim = first_dim(z)
+        for second in (1, 0):
+            keep = (0, second) if dim == 0 else (second, 0)
+            sent = (1, second) if dim == 0 else (second, 1)
+            index = blocks.index((keep[0], keep[1], z))
+            source = blocks.index((sent[0], sent[1], z))
+            peer = other_x if dim == 0 else other_y
+            sender.arrived(stage_pair.at[source], base + source, peer)
+            work[index] = (work[index].astype(jnp.float32) + stage_pair[source].astype(jnp.float32)).astype(jnp.bfloat16)
+            if second:
+                peer = other_y if dim == 0 else other_x
+                sender.send(work.at[index], stage_pair.at[index], base_second + index, peer)
+    base_z = 48
+    for z in range(4):
+        dim = first_dim(z)
+        crossed = (0, 1) if dim == 0 else (1, 0)
+        source = blocks.index((crossed[0], crossed[1], z))
+        index = blocks.index((0, 0, z))
+        peer = other_y if dim == 0 else other_x
+        sender.arrived(stage_pair.at[source], base_second + source, peer)
+        work[index] = (work[index].astype(jnp.float32) + stage_pair[source].astype(jnp.float32)).astype(jnp.bfloat16)
+    own_first = blocks.index((0, 0, 0))
+    for step in (3, 2, 1):
+        layer = place.layer(step)
+        sender.send(work.at[own_first + layer * 4], stage_z.at[step], base_z + step, place.device(z=layer))
+    total = work[own_first + place.z * 4].astype(jnp.float32)
+    for step in (1, 2, 3):
+        sender.arrived(stage_z.at[step], base_z + step, sibling)
+        total = total + stage_z[step].astype(jnp.float32)
+    dev_rows = chip_rows // 2
+    first, second = total[:dev_rows], total[dev_rows:]
+    is_first = place.core == 0
+    keep = jnp.where(is_first, first, second)
+    final[...] = jnp.where(is_first, second, first)
+    sender.send(final, stage_last, base_z + 4, sibling)
+    out_ref[:, mine] = keep
+    sender.arrived(stage_last, base_z + 4, sibling)
+    out_ref[:, other] = stage_last[...]
+    sender.close()
+
+
+def scatter_sums(part):
+    rows, width = part.shape
+    owners = lax.axis_size(("tower", "batch"))
+    half = width // 2
+    chip_rows = rows // 16
+    return pl.pallas_call(
+        scatter_kernel,
+        out_shape=jax.ShapeDtypeStruct((rows // owners, width), jnp.float32),
+        in_specs=[pl.BlockSpec(memory_space=pltpu.VMEM)],
+        out_specs=pl.BlockSpec(memory_space=pltpu.VMEM),
+        scratch_shapes=[
+            pltpu.VMEM((16, chip_rows, half), jnp.bfloat16),
+            pltpu.VMEM((16, chip_rows, half), jnp.bfloat16),
+            pltpu.VMEM((16, chip_rows, half), jnp.bfloat16),
+            pltpu.VMEM((4, chip_rows, half), jnp.bfloat16),
+            pltpu.VMEM((rows // owners, half), jnp.float32),
+            pltpu.VMEM((rows // owners, half), jnp.float32),
+            pltpu.SemaphoreType.DMA((34,)),
+            pltpu.SemaphoreType.DMA((56,)),
+        ],
+        compiler_params=pltpu.CompilerParams(
+            collective_id=2, has_side_effects=True, vmem_limit_bytes=48 * 2**20
+        ),
+    )(part)
+
+
+def fast(hidden_in, query_lengths, passage_lengths, positives, stored):
+    (query_weight, query_bias, key_weight, value_weight, value_bias, output_weight, output_bias, first_gain,
+     first_shift, inner_weight, inner_bias, outer_weight, outer_bias, second_gain, second_shift) = stored
+    micro, token_rows, width = hidden_in.shape[0], hidden_in.shape[2], hidden_in.shape[3]
+    inputs = hidden_in[:, 0]
+    side = lax.axis_index("tower")
+    batch = lax.axis_index("batch")
+    device = side * lax.axis_size("batch") + batch
+    is_query = side == 0
+    own_rows = query_weight.shape[0]
+    ff_rows = outer_weight.shape[0]
+    ff = inner_weight.shape[1]
+    head_size = width // HEADS
+    scale = head_size ** (-0.5)
+    vec_cols = jnp.stack(
+        [query_bias, value_bias, output_bias, first_gain, first_shift, outer_bias, second_gain, second_shift], 1
+    )
+    vec_cols = jnp.concatenate([vec_cols, inner_bias.reshape(-1, own_rows).T], 1)
+    vec_cols = jnp.pad(vec_cols, ((0, 0), (0, 128 - vec_cols.shape[1])))
+    cut = width // 2
+    inner_cut = 1152
+    wide = jnp.concatenate(
+        [query_weight, value_weight[:, :cut], vec_cols, key_weight, value_weight[:, cut:], jnp.zeros_like(vec_cols),
+         output_weight, inner_weight], 1)
+    wide = jnp.pad(wide, ((0, own_rows // 3), (0, 0)))
+    widths = (width + cut + 128, width + inner_cut)
+    all_wide, outer_mat = gather_weights(wide, outer_weight, widths)
+    query_mat = all_wide[:, :width]
+    vecs = all_wide[:, width + cut : width + cut + 12].astype(jnp.float32).T
+    key_mat = all_wide[:, widths[0] : widths[0] + width]
+    value_mat = jnp.concatenate(
+        [all_wide[:, width : width + cut], all_wide[:, widths[0] + width : widths[0] + width + cut]], 1)
+    out_mat = all_wide[:, 2 * widths[0] : 2 * widths[0] + width]
+    inner_mat = all_wide[:, 2 * widths[0] + width :]
+    query_vec, value_vec, out_vec, gain_one, shift_one, outer_vec, gain_two, shift_two = [vecs[i] for i in range(8)]
+    inner_vec = vecs[8:12].reshape(ff // ff_rows, -1, own_rows) if False else (
+        vecs[8:12].reshape(4, -1, own_rows).transpose(1, 0, 2).reshape(ff))
+    params = (query_mat, query_vec, key_mat, value_mat, value_vec, out_mat, out_vec, gain_one, shift_one, inner_mat,
+              inner_vec, outer_mat, outer_vec, gain_two, shift_two)
+
+    slot_count = query_lengths.shape[1]
+    passage_count = passage_lengths.shape[1]
+    passage_part = jnp.pad(passage_lengths, ((0, 0), (0, slot_count - passage_count)))
+    lengths = jnp.where(is_query, query_lengths, passage_part)
+    labels, valid, starts, live = jax.vmap(segments, (0, None))(lengths, token_rows)
+    flat = inputs.reshape(micro * token_rows, width)
+    queries = (product(flat, query_mat) + query_vec).astype(jnp.bfloat16).reshape(micro, token_rows, HEADS, head_size)
+    keys = product(flat, key_mat).astype(jnp.bfloat16).reshape(micro, token_rows, HEADS, head_size)
+    values = (product(flat, value_mat) + value_vec).astype(jnp.bfloat16).reshape(micro, token_rows, HEADS, head_size)
+    allowed = labels[:, None, :, None] == labels[:, None, None, :]
+    scores = jnp.einsum("mqhd,mkhd->mhqk", queries, keys, preferred_element_type=jnp.float32) * scale
+    scores = jnp.where(allowed, scores, MASKED)
+    highest = jnp.max(scores, -1, keepdims=True)
+    powers = jnp.exp(scores - highest)
+    shares = (powers / jnp.sum(powers, -1, keepdims=True)).astype(jnp.bfloat16)
+    attended = jnp.einsum("mhqk,mkhd->mqhd", shares, values, preferred_element_type=jnp.float32)
+    attended = attended.astype(jnp.bfloat16).reshape(micro, token_rows, width)
+    result, unused = tail(flat, attended.reshape(micro * token_rows, width), params)
+    shown = jnp.where(valid.reshape(-1)[:, None], result, 0.0).astype(jnp.bfloat16)
+    hidden_out = shown.reshape(micro, 1, token_rows, width)
+
+    row_inputs = jnp.take_along_axis(inputs, starts[:, :, None], 1)
+    row_attended = jnp.take_along_axis(attended, starts[:, :, None], 1)
+    both = jnp.concatenate([row_inputs, row_attended], 2)
+    query_block = jnp.concatenate([both[0], both[1], jnp.zeros((BLOCK - 2 * slot_count, 2 * width), both.dtype)], 0)
+    coded = jnp.pad(positives.astype(both.dtype), ((0, 0), (0, 2 * width - slot_count)))
+    passage_block = jnp.concatenate(
+        [jnp.zeros((2 * slot_count, 2 * width), both.dtype), both[0, :passage_count], both[1, :passage_count], coded], 0)
+    block = jnp.where(is_query, query_block, passage_block)
+    nothing = jnp.zeros_like(block)
+    first_core = batch % 2 == 0
+    block = jnp.concatenate([jnp.where(first_core, block, nothing), jnp.where(first_core, nothing, block)], 0)
+    cls = gather_cls(block)
+
+    count = cls.shape[0]
+    place = jnp.arange(count, dtype=jnp.int32) % BLOCK
+    group = jnp.arange(count, dtype=jnp.int32) // BLOCK
+    query_row = place < micro * slot_count
+    passage_row = (place >= micro * slot_count) & (place < micro * (slot_count + passage_count))
+    row_micro = jnp.where(query_row, place // slot_count, (place - micro * slot_count) // passage_count)
+    used = query_row | passage_row
+    codes = cls.reshape(-1, BLOCK, 2 * width)[:, micro * (slot_count + passage_count) :, :slot_count]
+    codes = jnp.pad(codes.reshape(-1, micro * slot_count), ((0, 0), (0, BLOCK - micro * slot_count)))
+    codes = codes.reshape(count).astype(jnp.int32)
+    target_col = BLOCK * (codes // passage_count) + micro * slot_count + row_micro * passage_count + codes % passage_count
+    cls_in = jnp.where(used[:, None], cls[:, :width], 0)
+    cls_att = jnp.where(used[:, None], cls[:, width:], 0)
+    result, kept = tail(cls_in, cls_att, params)
+    normed_one, inverse_one, hidden_low, inner, active, normed_two, inverse_two = kept
+    vectors = result.astype(jnp.bfloat16)
+    cls_scale = width ** (-0.5)
+    logits = product_nt(vectors, vectors) * cls_scale
+    paired = query_row[:, None] & passage_row[None, :] & (row_micro[:, None] == row_micro[None, :])
+    logits = jnp.where(paired, logits, MASKED)
+    powers = jnp.where(paired, jnp.exp(logits - jnp.max(logits, -1, keepdims=True)), 0.0)
+    total = jnp.sum(powers, -1, keepdims=True)
+    hit = (jnp.arange(count, dtype=jnp.int32)[None, :] == target_col[:, None]) & paired
+    grad_logits = (powers / jnp.where(total > 0, total, 1.0) - hit.astype(jnp.float32)) / micro
+    grad_logits = grad_logits.astype(jnp.bfloat16)
+    upstream = (product(grad_logits, vectors) + product_tn(grad_logits, vectors)) * cls_scale
+
+    grad_sum_two, grad_gain_two, grad_shift_two = normalize_back(upstream, normed_two, inverse_two, gain_two)
+    grad_outer = grad_sum_two.astype(jnp.bfloat16)
+    grad_outer_vec = jnp.sum(grad_outer.astype(jnp.float32), 0)
+    grad_inner = (product_nt(grad_outer, outer_mat) * gelu_slope(inner)).astype(jnp.bfloat16)
+    grad_inner_vec = jnp.sum(grad_inner.astype(jnp.float32), 0)
+    grad_hidden = grad_sum_two + product_nt(grad_inner, inner_mat)
+    grad_sum_one, grad_gain_one, grad_shift_one = normalize_back(grad_hidden, normed_one, inverse_one, gain_one)
+    grad_branch = grad_sum_one.astype(jnp.bfloat16)
+    grad_out_vec = jnp.sum(grad_branch.astype(jnp.float32), 0)
+
+    def own_columns(array, columns):
+        return lax.dynamic_slice_in_dim(array, device * columns, columns, 1)
+
+    def own_part(vector, length):
+        return lax.dynamic_slice_in_dim(vector, device * length, length, 0)
+
+    grad_outer_mat = product_tn(own_columns(active, ff_rows), grad_outer)
+    grad_inner_mat = product_tn(own_columns(hidden_low, own_rows), grad_inner)
+    grad_out_mat = product_tn(own_columns(cls_att, own_rows), grad_branch)
+
+    def own_slots(array):
+        rows = lax.dynamic_slice_in_dim(array, batch * BLOCK, BLOCK, 0)
+        ours = rows[: micro * slot_count].reshape(micro, slot_count, width)
+        theirs = rows[micro * slot_count : micro * (slot_count + passage_count)].reshape(micro, passage_count, width)
+        theirs = jnp.pad(theirs, ((0, 0), (0, slot_count - passage_count), (0, 0)))
+        return jnp.where(live[:, :, None], jnp.where(is_query, ours, theirs), 0)
+
+    own_branch = own_slots(grad_branch)
+    own_sum_one = own_slots(grad_sum_one)
+    grad_attended = product_nt(own_branch.reshape(-1, width), out_mat).astype(jnp.bfloat16)
+    grad_attended = grad_attended.reshape(micro, slot_count, HEADS, head_size)
+    row_queries = jnp.take_along_axis(queries, starts[:, :, None, None], 1)
+    row_labels = jnp.take_along_axis(labels, starts, 1)
+    row_allowed = row_labels[:, None, :, None] == labels[:, None, None, :]
+    scores = jnp.einsum("mrhd,mthd->mhrt", row_queries, keys, preferred_element_type=jnp.float32) * scale
+    scores = jnp.where(row_allowed, scores, MASKED)
+    powers = jnp.exp(scores - jnp.max(scores, -1, keepdims=True))
+    shares = powers / jnp.sum(powers, -1, keepdims=True)
+    shares_low = shares.astype(jnp.bfloat16)
+    grad_shares = jnp.einsum("mrhd,mthd->mhrt", grad_attended, values, preferred_element_type=jnp.float32)
+    grad_scores = (shares * (grad_shares - jnp.sum(grad_shares * shares, -1, keepdims=True))).astype(jnp.bfloat16)
+    grad_queries = jnp.einsum("mhrt,mthd->mrhd", grad_scores, keys, preferred_element_type=jnp.float32) * scale
+    grad_queries = grad_queries.astype(jnp.bfloat16).reshape(micro, slot_count, width)
+    grad_keys = jnp.einsum("mhrt,mrhd->mthd", grad_scores, row_queries, preferred_element_type=jnp.float32) * scale
+    grad_keys = grad_keys.astype(jnp.bfloat16).reshape(micro * token_rows, width)
+    grad_values = jnp.einsum("mhrt,mrhd->mthd", shares_low, grad_attended, preferred_element_type=jnp.float32)
+    grad_values = grad_values.astype(jnp.bfloat16).reshape(micro * token_rows, width)
+    grad_inputs = product_nt(grad_keys, key_mat) + product_nt(grad_values, value_mat)
+    grad_rows = product_nt(grad_queries.reshape(-1, width), query_mat) + own_sum_one.reshape(-1, width)
+    row_index = (starts + jnp.arange(micro, dtype=jnp.int32)[:, None] * token_rows).reshape(-1)
+    grad_inputs = grad_inputs.at[row_index].add(grad_rows)
+    input_grad = grad_inputs.astype(jnp.bfloat16).reshape(micro, 1, token_rows, width)
+    lanes = jnp.arange(128, dtype=jnp.int32)[None, :]
+    flat_queries = grad_queries.reshape(-1, width)
+    sums = product_tn(flat_queries, jnp.broadcast_to(lanes == 0, (flat_queries.shape[0], 128)).astype(jnp.bfloat16))
+    sums = sums + product_tn(grad_values, jnp.broadcast_to(lanes == 1, (grad_values.shape[0], 128)).astype(jnp.bfloat16))
+    partial = jnp.concatenate(
+        [product_tn(row_inputs.reshape(-1, width), flat_queries), product_tn(flat, grad_keys),
+         product_tn(flat, grad_values), sums, jnp.zeros_like(sums)], 1).astype(jnp.bfloat16)
+    shard = scatter_sums(partial)
+    return (
+        hidden_out,
+        input_grad,
+        shard[:, :width],
+        shard[:, 3 * width],
+        shard[:, width : 2 * width],
+        shard[:, 2 * width : 3 * width],
+        shard[:, 3 * width + 1],
+        grad_out_mat,
+        own_part(grad_out_vec, own_rows),
+        own_part(grad_gain_one, own_rows),
+        own_part(grad_shift_one, own_rows),
+        grad_inner_mat,
+        own_part(grad_inner_vec, ff_rows),
+        grad_outer_mat,
+        own_part(grad_outer_vec, own_rows),
+        own_part(grad_gain_two, own_rows),
+        own_part(grad_shift_two, own_rows),
+    )
 
 
 def local(
@@ -262,6 +830,8 @@
         second_gain,
         second_shift,
     )
+    if lax.axis_size("tower") == 2 and lax.axis_size("batch") == 16 and hidden_in.shape[3] == 768:
+        return fast(hidden_in, query_lengths, passage_lengths, positives, stored)
     micro = hidden_in.shape[0]
     width = hidden_in.shape[3]
     cls_scale = width ** (-0.5)

time: 1020 us -> 448 us (0.44)
  waiting for transfers between devices: 468 us -> 0 us
  Pallas kernels: 0 us -> 147 us
  blocking collectives: 138 us -> 0 us
  local copies, waits for them, and re-layouts: 114 us -> 91.6 us
  starting transfers between devices: 22.1 us -> 0 us
  matrix products: 186 us -> 168 us
  loops' own time: 16.6 us -> 0 us
  between operations: 18.2 us -> 2.28 us
  other arithmetic: 46.6 us -> 31.5 us
    pallas_call x0 -> x3, Pallas kernels: none -> 147 us  [the longest x1 84.3 us: gather_weights(): pl.pallas_call(functools.partial(gather_kernel, widths), out_shape=(jax.S...]
    reduce_scatter x4 -> x0, waiting for transfers between devices: 142 us -> none  [local(): lax.psum_scatter(half_totals, 'batch', scatter_dimension=0, tiled=True)]
    ppermute x21 -> x0, waiting for transfers between devices: 128 us -> none  [partner_2(): lax.ppermute(x, axis, [(i, i ^ 1 << apart) for i in range(lax.axis_size(a...]
    all_gather x6 -> x0, waiting for transfers between devices: 109 us -> none  [the longest x1 53 us: local(): lax.all_gather(query_weight, ('tower', 'batch'), axis=0, tiled=True)]
    unnamed x2 -> x0, blocking collectives: 100 us -> none
    unnamed x16 -> x0, waiting for transfers between devices: 88.9 us -> none
    all_gather x2 -> x0, blocking collectives: 37.8 us -> none  [local(): pooled = lax.all_gather(passage_cls, 'batch', axis=0, tiled=True)]
    reshape x4 -> x18, local copies, waits for them, and re-layouts: 0.5 us -> 27 us  [the longest x2 7.33 us: fast(): (product(flat, query_mat) + query_vec).astype(jnp.bfloat16)]
  transfers between devices with their start and end apart: 34 -> 0, of which waited for: 16 -> 0; matrix products, arithmetic and copies ran while one was open for 26% -> 0% of each run, Pallas kernels for 0% -> 0%
where the time goes in v1:
time: 448 us; the launch traced here: 441 us
  matrix products  168 us (38%)
  Pallas kernels  147 us (33%)
  local copies, waits for them, and re-layouts  91.6 us (20%)
  other arithmetic  31.5 us (7%)
    dot_general x10, matrix products, product(): return jnp.dot(left, right, preferred_element_type=jnp.float32)  86.3 us
    pallas_call x1, Pallas kernels, gather_weights(): pl.pallas_call(functools.partial(gather_kernel, widths), out_shape=(jax.S...  84.3 us
    pallas_call x1, Pallas kernels, scatter_sums(): pl.pallas_call(scatter_kernel, out_shape=jax.ShapeDtypeStruct((rows // ow...  38.6 us
    dot_general x7, matrix products, product_nt(): jnp.einsum('ra,ba->rb', left, right, preferred_element_type=jnp.float32)  30.3 us
    pallas_call x1, Pallas kernels, gather_cls(): pl.pallas_call(cls_kernel, out_shape=jax.ShapeDtypeStruct((rows * chips,...  24.5 us
    unnamed x182, local copies, waits for them, and re-layouts  18.9 us
    dot_general x9, matrix products, product_tn(): jnp.einsum('ta,tb->ab', left, right, preferred_element_type=jnp.float32)  17.2 us
    sub x1, matrix products, fast(): powers = jnp.exp(scores - highest)  15 us

profile of v1, /device:TPU:0, one launch (start us, length us, event | category | flops | bytes accessed | tf_op | source)
XLA Modules:
  0.0 441.2 jit_solution(14918212052450544615)
XLA Ops:
  13.3 84.3 %shard_map.314 = (bf16[768,6400]{1,0:T(8,128)(2,1)}, bf16[3072,768]{1,0:T(8,128)(2,1)S(1)}) custom-call(bf16[32,6400]{1,0:T(8,128)(2,1)S(1)} %pad.30.wide_ref, bf16[96,768]{1,0:T(8,128)(2,1)S(1)} %copy-done), custom_call_target="tpu_custom_call" | custom-call | tf_op jit(solution)/shard_map/pallas_call | solution.py:422
  110.2 4.9 %fusion.61 = bf16[1024,768]{0,1:T(8,128)(2,1)} fusion(bf16[1024,768]{1,0:T(8,128)(2,1)} %bitcast.145, bf16[768,6400]{1,0:T(8,128)(2,1)} %get-tuple-element.20), kind=kOutput, calls=%fused_computation.117 | convolution fusion | flops 1208745984 | bytes 4325376 | tf_op jit(solution)/shard_map/dot_general | solution.py:26
  118.0 15.0 %fusion.195 = (f32[2,12,512]{2,1,0:T(8,128)}, f32[2,12,512,512]{2,3,1,0:T(8,128)}) fusion(pred[2,512,512]{1,2,0:T(8,128)(4,1)} %broadcast_compare_fusion, bf16[2,512,12,64]{1,0,3,2:T(2,128)(2,1)S(1)} %reshape.405, bf16[2,512,12,64]{1,0,3,2:T(2,128)(2,1)S(1)} %reshape.406), kind=kOutput, calls=%fused_computation.344 | convolution fusion | flops 830472704 | bytes 28884992 | tf_op jit(solution)/shard_map/sub | solution.py:666
  135.4 4.1 fusion.63
  142.4 10.2 %fusion.49 = bf16[2,12,64,512]{3,2,1,0:T(8,128)(2,1)S(1)} fusion(f32[2,12,512,512]{2,3,1,0:T(8,128)} %get-tuple-element.118, f32[2,12,512]{2,1,0:T(8,128)} %get-tuple-element.117, bf16[2,512,12,64]{1,0,3,2:T(2,128)(2,1)S(1)} %reshape.404), kind=kOutput, calls=%fused_computation.98 | convolution fusion | flops 818675712 | bytes 28360704 | tf_op jit(solution)/shard_map/mhqk,mkhd->mqhd/dot_general | solution.py:668
  159.8 35.5 %fusion.48.clone.4 = bf16[1024,3072]{1,0:T(8,128)(2,1)S(1)} fusion(f32[3072]{0:T(1024)S(1)} %add.378, bf16[768,6400]{1,0:T(8,128)(2,1)} %get-tuple-element.20, f32[1024,768]{1,0:T(8,128)} %copy-done.21, f32[768]{0:T(1024)S(1)} %get-tuple-element.84, f32[768]{0:T(1024)S(1)} %get-tuple-element.85, ...), kind=kOutput, calls=%fused_computation.14.clone.clone.clone.clone.clone.clone.1 | convolution fusion | flops 5043388416 | bytes 14182400 | tf_op jit(solution)/shard_map/dot_general | solution.py:26
  195.4 5.4 %fusion.209 = (f32[1024]{0:T(1024)S(1)}, f32[1024,768]{1,0:T(8,128)S(1)}) fusion(f32[768]{0:T(1024)S(1)} %get-tuple-element.83, bf16[3072,768]{1,0:T(8,128)(2,1)S(1)} %bitcast.124, f32[1024,768]{1,0:T(8,128)S(1)} %copy-done.22, f32[768]{0:T(1024)S(1)} %get-tuple-element.84, f32[768]{0:T(1024)S(1)} %get-tuple-element.85, f32[1024]{0:T(1024)S(1)} %add_rsqrt_fusion.3, ...), kind=kOutput, calls=%fused_computation.350 | convolution fusion | flops 4838915072 | bytes 17323008 | tf_op jit(solution)/shard_map/dot_general | solution.py:26
  203.3 3.4 select_convert_fusion
  208.8 6.0 %copy.112 = bf16[2,512,12,64]{3,2,1,0:T(8,128)(2,1)} copy(bf16[2,512,12,64]{1,0,3,2:T(2,128)(2,1)S(1)} %copy-done.16) | data formatting | bytes 3145728 | tf_op jit(solution)/shard_map/reshape | solution.py:659
  228.5 24.5 %shard_map.315 = bf16[640,1536]{1,0:T(8,128)(2,1)S(1)} custom-call(bf16[80,1536]{1,0:T(8,128)(2,1)S(1)} %pad_maximum_fusion.3.block_ref), custom_call_target="tpu_custom_call" | custom-call | tf_op jit(solution)/shard_map/pallas_call | solution.py:487
  257.3 22.8 %fusion.19 = (bf16[640,3072]{1,0:T(8,128)(2,1)S(1)}, f32[640,3072]{1,0:T(8,128)}) fusion(f32[3072]{0:T(1024)S(1)} %copy-done.59, bf16[640,768]{1,0:T(8,128)(2,1)S(1)} %add_convert_fusion.4, bf16[768,6400]{1,0:T(8,128)(2,1)} %get-tuple-element.20), kind=kOutput, calls=%fused_computation.38 | convolution fusion | flops 3149660160 | bytes 17510400 | tf_op jit(solution)/shard_map/dot_general | solution.py:26
  280.2 3.4 fusion.205
  292.0 3.7 fusion.206
  302.6 6.7 %convert_reduce_fusion = (f32[3072]{0:T(1024)}, bf16[640,3072]{1,0:T(8,128)(2,1)S(1)}) fusion(f32[640,3072]{1,0:T(8,128)S(1)} %bitcast.162, f32[3072]{0:T(1024)S(1)} %copy-done.60, bf16[3072,768]{1,0:T(8,128)(2,1)S(1)} %bitcast.128, f32[640,768]{1,0:T(8,128)S(1)} %get-tuple-element.92), kind=kOutput, calls=%fused_computation.45 | convolution fusion | flops 3045946368 | bytes 18505728 | tf_op jit(solution)/shard_map/ra,ba->rb/dot_general | solution.py:34
  309.4 8.2 %multiply_reduce_fusion.3 = (f32[768]{0:T(1024)}, f32[640]{0:T(1024)S(1)}, f32[640]{0:T(1024)S(1)}, f32[768]{0:T(1024)}, f32[640,768]{1,0:T(8,128)S(1)}) fusion(f32[640,768]{1,0:T(8,128)S(1)} %copy-done.5, f32[640]{0:T(1024)S(1)} %copy-done.49, f32[640]{0:T(1024)S(1)} %copy-done.41, f32[768]{0:T(1024)S(1)} %copy-done.44, ...), kind=kOutput, calls=%fused_computation.80 | convolution fusion | flops 3024811264 | bytes 14568448 | tf_op jit(solution)/shard_map/ra,ba->rb/dot_general | solution.py:34
  340.6 4.4 fusion.90
  345.0 4.3 fusion.62
  349.3 3.2 copy.121
  353.2 3.2 convolution_add_fusion
  369.1 4.4 scatter_fusion
  373.4 3.2 convert_element_type.187
  377.2 3.5 fusion.70
  383.2 38.6 %shard_map.316 = f32[24,2560]{1,0:T(8,128)S(1)} custom-call(bf16[768,2560]{1,0:T(8,128)(2,1)S(1)} %broadcast_dynamic-update-slice_fusion.part_ref), custom_call_target="tpu_custom_call" | custom-call | tf_op jit(solution)/shard_map/pallas_call | solution.py:592
  430.2 3.7 fusion.109
  (325 shorter events, 132.5 us)
Async XLA Ops:
  0.7 102.3 %copy-start.72 = (s32[2,17]{1,0:T(2,128)S(1)}, s32[2,17]{1,0:T(2,128)}, u32[]{:S(2)}) copy-start(s32[2,17]{1,0:T(2,128)} %param.22) | copy-start | bytes 412
  0.7 102.3 %copy-start.73 = (s32[2,2]{1,0:T(2,128)S(1)}, s32[2,2]{1,0:T(2,128)}, u32[]{:S(2)}) copy-start(s32[2,2]{1,0:T(2,128)} %param.23) | copy-start | bytes 52
  13.3 92.7 %copy-start.37 = (bf16[2,1,512,768]{3,2,1,0:T(8,128)(2,1)S(1)}, bf16[2,1,512,768]{3,2,1,0:T(8,128)(2,1)}, u32[]{:S(2)}) copy-start(bf16[2,1,512,768]{3,2,1,0:T(8,128)(2,1)} %param.21) | copy-start | bytes 4718596
  102.9 51.7 %copy-start.69 = (f32[768]{0:T(1024)}, f32[768]{0:T(1024)S(1)}, u32[]{:S(2)}) copy-start(f32[768]{0:T(1024)S(1)} %get-tuple-element.86) | copy-start | bytes 9220
  102.9 92.4 %copy-start.42 = (f32[768]{0:T(1024)}, f32[768]{0:T(1024)S(1)}, u32[]{:S(2)}) copy-start(f32[768]{0:T(1024)S(1)} %get-tuple-element.85) | copy-start | bytes 9220
  102.9 92.4 %copy-start.52 = (f32[768]{0:T(1024)}, f32[768]{0:T(1024)S(1)}, u32[]{:S(2)}) copy-start(f32[768]{0:T(1024)S(1)} %get-tuple-element.84) | copy-start | bytes 9220
  102.9 92.4 %copy-start.67 = (f32[768]{0:T(1024)}, f32[768]{0:T(1024)S(1)}, u32[]{:S(2)}) copy-start(f32[768]{0:T(1024)S(1)} %get-tuple-element.83) | copy-start | bytes 9220
  110.2 7.8 %copy-start.15 = (bf16[2,512,12,64]{1,0,3,2:T(2,128)(2,1)}, bf16[2,512,12,64]{1,0,3,2:T(2,128)(2,1)S(1)}, u32[]{:S(2)}) copy-start(bf16[2,512,12,64]{1,0,3,2:T(2,128)(2,1)S(1)} %reshape.405) | copy-start | bytes 4718596
  142.3 10.2 %copy-start.24 = (bf16[2,512,12,64]{1,0,3,2:T(2,128)(2,1)}, bf16[2,512,12,64]{1,0,3,2:T(2,128)(2,1)S(1)}, u32[]{:S(2)}) copy-start(bf16[2,512,12,64]{1,0,3,2:T(2,128)(2,1)S(1)} %reshape.404) | copy-start | bytes 4718596
  154.7 40.7 %slice-start = ((s8[4718592]{0:T(1024)(128)(4,1)}), s8[524288]{0:T(1024)(128)(4,1)S(1)}, s32[]{:S(2)}) async-start(s8[4718592]{0:T(1024)(128)(4,1)} %bitcast.123), calls=%async_computation | async-start | bytes 1048576
  159.8 35.6 %copy-start.58 = (f32[3072]{0:T(1024)}, f32[3072]{0:T(1024)S(1)}, u32[]{:S(2)}) copy-start(f32[3072]{0:T(1024)S(1)} %add.378) | copy-start | bytes 36868
  159.8 35.6 %slice-start.1 = ((s8[4718592]{0:T(1024)(128)(4,1)}), s8[4194304]{0:T(1024)(128)(4,1)S(1)}, s32[]{:S(2)}) async-start(s8[4718592]{0:T(1024)(128)(4,1)} %bitcast.123), calls=%async_computation.1 | async-start | bytes 8388608
  159.8 35.6 %copy-start.22 = (f32[1024,768]{1,0:T(8,128)S(1)}, f32[1024,768]{1,0:T(8,128)}, u32[]{:S(2)}) copy-start(f32[1024,768]{1,0:T(8,128)} %copy-done.21) | copy-start | bytes 9437188
  255.5 24.7 %copy-start.4 = (f32[640,768]{1,0:T(8,128)}, f32[640,768]{1,0:T(8,128)S(1)}, u32[]{:S(2)}) copy-start(f32[640,768]{1,0:T(8,128)S(1)} %get-tuple-element.120) | copy-start | bytes 5898244
  255.5 24.7 %slice-start.2 = ((s8[4718592]{0:T(1024)(128)(4,1)}), s8[4194304]{0:T(1024)(128)(4,1)S(1)}, s32[]{:S(2)}) async-start(s8[4718592]{0:T(1024)(128)(4,1)} %bitcast.125), calls=%async_computation.2 | async-start | bytes 8388608
  257.3 22.9 %copy-start.28 = (bf16[640,768]{1,0:T(8,128)(2,1)}, bf16[640,768]{1,0:T(8,128)(2,1)S(1)}, u32[]{:S(2)}) copy-start(bf16[640,768]{1,0:T(8,128)(2,1)S(1)} %add_convert_fusion.4) | copy-start | bytes 2949124
  257.3 22.9 %slice-start.3 = ((s8[4718592]{0:T(1024)(128)(4,1)}), s8[524288]{0:T(1024)(128)(4,1)S(1)}, s32[]{:S(2)}) async-start(s8[4718592]{0:T(1024)(128)(4,1)} %bitcast.125), calls=%async_computation.3 | async-start | bytes 1048576
  257.3 22.9 %copy-start.68 = (f32[768]{0:T(1024)S(1)}, f32[768]{0:T(1024)}, u32[]{:S(2)}) copy-start(f32[768]{0:T(1024)} %copy-done.67) | copy-start | bytes 9220
  309.3 8.2 %copy-start.20 = (bf16[640,3072]{1,0:T(8,128)(2,1)}, bf16[640,3072]{1,0:T(8,128)(2,1)S(1)}, u32[]{:S(2)}) copy-start(bf16[640,3072]{1,0:T(8,128)(2,1)S(1)} %get-tuple-element.138) | copy-start | bytes 11796484
  353.2 9.1 %copy-start.66 = (pred[2,17]{1,0:T(4,128)(4,1)S(1)}, pred[2,17]{1,0:T(4,128)(4,1)}, u32[]{:S(2)}) copy-start(pred[2,17]{1,0:T(4,128)(4,1)} %get-tuple-element.100) | copy-start | bytes 106
  367.2 9.4 %copy-start.35 = (bf16[34,768]{1,0:T(8,128)(2,1)}, bf16[34,768]{1,0:T(8,128)(2,1)S(1)}, u32[]{:S(2)}) copy-start(bf16[34,768]{1,0:T(8,128)(2,1)S(1)} %reshape_reshape.8) | copy-start | bytes 156676
  382.4 40.7 %copy-start.71 = (pred[640]{0:T(1024)(128)(4,1)S(1)}, pred[640]{0:T(1024)(128)(4,1)}, u32[]{:S(2)}) copy-start(pred[640]{0:T(1024)(128)(4,1)} %copy-done.70) | copy-start | bytes 1924
  383.1 41.1 %copy-start.19 = (bf16[640,768]{1,0:T(8,128)(2,1)S(1)}, bf16[640,768]{1,0:T(8,128)(2,1)}, u32[]{:S(2)}) copy-start(bf16[640,768]{1,0:T(8,128)(2,1)} %get-tuple-element.94) | copy-start | bytes 2949124
  424.3 10.9 %copy-start.8 = (f32[640,768]{1,0:T(8,128)S(1)}, f32[640,768]{1,0:T(8,128)}, u32[]{:S(2)}) copy-start(f32[640,768]{1,0:T(8,128)} %copy-done.7) | copy-start | bytes 5898244
  (62 other events, 204.7 us)

commit v2 on v0

--- a/solution.py
+++ b/solution.py
@@ -1,6 +1,8 @@
 import jax
 import jax.numpy as jnp
 from jax import lax
+from jax.experimental import pallas as pl
+from jax.experimental.pallas import tpu as pltpu
 from jax.sharding import PartitionSpec as P
 
 HEADS = 12
@@ -222,6 +224,759 @@
         keep_list.append(lax.dynamic_slice_in_dim(item, side * half, half, 0))
         give_list.append(lax.dynamic_slice_in_dim(item, (1 - side) * half, half, 0))
     return (tuple(keep_list), tuple(give_list))
+
+
+MESH = pl.DeviceIdType.MESH
+BLOCK = 40
+QS, PS, STREAM, WIDTH, FF, MICRO = 17, 2, 512, 768, 3072, 2
+ROWS = MICRO * STREAM
+CLS = 16 * BLOCK
+HALF = 1280
+PART = (HALF, 1920)
+OWN = 24
+FF_OWN = 96
+BF, F32 = jnp.bfloat16, jnp.float32
+
+
+class Place:
+    def __init__(self):
+        self.x = lax.axis_index("tower")
+        self.batch = lax.axis_index("batch")
+        self.core = self.batch % 2
+        self.y = (self.batch // 2) % 2
+        self.z = self.batch // 4
+        self.index = self.x * 16 + self.batch
+
+    def device(self, x=None, y=None, z=None, core=None):
+        x = self.x if x is None else x
+        y = self.y if y is None else y
+        z = self.z if z is None else z
+        core = self.core if core is None else core
+        return (x, z * 4 + y * 2 + core)
+
+    def chip(self, x=None, y=None, z=None):
+        x = self.x if x is None else x
+        y = self.y if y is None else y
+        z = self.z if z is None else z
+        return x * 8 + z * 2 + y
+
+    def layer(self, step):
+        if step == 0:
+            return self.z
+        if step == 1:
+            return self.z + 1 - 2 * (self.z % 2)
+        if step == 2:
+            return (self.z + 2) % 4
+        return 3 - self.z
+
+    @property
+    def sibling(self):
+        return self.device(core=1 - self.core)
+
+    @property
+    def over_x(self):
+        return self.device(x=1 - self.x)
+
+    @property
+    def over_y(self):
+        return self.device(y=1 - self.y)
+
+
+def greet(place):
+    barrier = pltpu.get_barrier_semaphore()
+    peers = [place.device(z=place.layer(step)) for step in (1, 2, 3)]
+    peers += [place.over_x, place.over_y, place.sibling]
+    for peer in peers:
+        pl.semaphore_signal(barrier, inc=1, device_id=peer, device_id_type=MESH)
+    pl.semaphore_wait(barrier, len(peers))
+
+
+class Sender:
+    def __init__(self, place, send_sems, recv_sems):
+        self.place = place
+        self.send_sems = send_sems
+        self.recv_sems = recv_sems
+        self.used = 0
+        self.open = []
+
+    def send(self, src, dst, slot, peer):
+        copy = pltpu.make_async_remote_copy(
+            src_ref=src,
+            dst_ref=dst,
+            send_sem=self.send_sems.at[self.used],
+            recv_sem=self.recv_sems.at[slot],
+            device_id=peer,
+            device_id_type=MESH,
+        )
+        self.used += 1
+        copy.start()
+        self.open.append(copy)
+
+    def arrived(self, dst, slot):
+        pltpu.make_async_remote_copy(
+            src_ref=dst,
+            dst_ref=dst,
+            send_sem=self.send_sems.at[0],
+            recv_sem=self.recv_sems.at[slot],
+            device_id=self.place.sibling,
+            device_id_type=MESH,
+        ).wait_recv()
+
+    def close(self):
+        for copy in self.open:
+            copy.wait_send()
+        self.open = []
+
+
+def tile(index, size, unit):
+    return pl.ds(pl.multiple_of(index * unit, unit), size)
+
+
+def loop(count, body):
+    def step(index, carry):
+        body(index)
+        return carry
+
+    lax.fori_loop(0, count, step, 0)
+
+
+def dot(left, right):
+    return jnp.dot(left, right, preferred_element_type=F32)
+
+
+def dot_nt(left, right):
+    return lax.dot_general(left, right, (((1,), (1,)), ((), ())), preferred_element_type=F32)
+
+
+def dot_tn(left, right):
+    return lax.dot_general(left, right, (((0,), (0,)), ((), ())), preferred_element_type=F32)
+
+
+def iota(shape, dim):
+    return lax.broadcasted_iota(jnp.int32, shape, dim)
+
+
+def centre(values):
+    average = jnp.mean(values, -1, keepdims=True)
+    centred = values - average
+    inverse = lax.rsqrt(jnp.mean(centred * centred, -1, keepdims=True) + EPSILON)
+    return centred * inverse, inverse
+
+
+def centre_back(scaled, normed, inverse):
+    return inverse * (
+        scaled - jnp.mean(scaled, -1, keepdims=True) - normed * jnp.mean(scaled * normed, -1, keepdims=True)
+    )
+
+
+def weight_steps(place, sender, all_wide, all_tall):
+    def view(chunk, core, chip):
+        if chunk < 2:
+            first = pl.multiple_of((0, 2 * HALF)[chunk] + core * PART[chunk], 128)
+            return all_wide.at[tile(chip, 2 * OWN, 2 * OWN), pl.ds(first, PART[chunk])]
+        return all_tall.at[tile(chip * 2 + core, FF_OWN, FF_OWN), :]
+
+    def slot(chunk, kind, layer):
+        return (chunk * 8 + kind) * 4 + layer
+
+    def begin(chunk):
+        own = view(chunk, place.core, place.chip())
+        for step in (3, 2, 1):
+            sender.send(own, own, slot(chunk, 0, place.z), place.device(z=place.layer(step)))
+        sender.send(own, own, slot(chunk, 1, place.z), place.over_x)
+        sender.send(own, own, slot(chunk, 2, place.z), place.over_y)
+        sender.send(own, own, slot(chunk, 4, place.z), place.sibling)
+
+    def along(chunk):
+        for step in (1, 2, 3):
+            layer = place.layer(step)
+            block = view(chunk, place.core, place.chip(z=layer))
+            sender.arrived(block, slot(chunk, 0, layer))
+            sender.send(block, block, slot(chunk, 1, layer), place.over_x)
+            sender.send(block, block, slot(chunk, 2, layer), place.over_y)
+            sender.send(block, block, slot(chunk, 4, layer), place.sibling)
+            yield
+
+    def across(chunk):
+        for step in range(4):
+            layer = place.layer(step)
+            from_x = view(chunk, place.core, place.chip(x=1 - place.x, z=layer))
+            sender.arrived(from_x, slot(chunk, 1, layer))
+            if step < 2:
+                sender.send(from_x, from_x, slot(chunk, 3, layer), place.over_y)
+            sender.send(from_x, from_x, slot(chunk, 5, layer), place.sibling)
+            from_y = view(chunk, place.core, place.chip(y=1 - place.y, z=layer))
+            sender.arrived(from_y, slot(chunk, 2, layer))
+            if step >= 2:
+                sender.send(from_y, from_y, slot(chunk, 3, layer), place.over_x)
+            sender.send(from_y, from_y, slot(chunk, 6, layer), place.sibling)
+            yield
+
+    def corner(chunk):
+        for step in range(4):
+            layer = place.layer(step)
+            block = view(chunk, place.core, place.chip(x=1 - place.x, y=1 - place.y, z=layer))
+            sender.arrived(block, slot(chunk, 3, layer))
+            sender.send(block, block, slot(chunk, 7, layer), place.sibling)
+            yield
+
+    def twin(chunk):
+        for step in range(4):
+            layer = place.layer(step)
+            for kind, x, y in ((4, 0, 0), (5, 1, 0), (6, 0, 1), (7, 1, 1)):
+                chip = place.chip(x=1 - place.x if x else place.x, y=1 - place.y if y else place.y, z=layer)
+                sender.arrived(view(chunk, 1 - place.core, chip), slot(chunk, kind, layer))
+        yield
+
+    return begin, along, across, corner, twin
+
+
+def cls_steps(place, sender, base, block_ref, merged, stage, out_ref):
+    rows, half = 2 * BLOCK, WIDTH
+    mine = tile(place.core, half, half)
+    other = tile(1 - place.core, half, half)
+
+    def view(core, y, z):
+        return out_ref.at[tile(z * 2 + y, rows, rows), tile(core, half, half)]
+
+    sender.send(block_ref.at[:, other], stage.at[0], base, place.sibling)
+    yield
+    sender.arrived(stage.at[0], base)
+    merged[...] = (block_ref[:, mine].astype(F32) + stage[0].astype(F32)).astype(BF)
+    sender.send(merged, stage.at[1], base + 1, place.over_x)
+    yield
+    sender.arrived(stage.at[1], base + 1)
+    own = view(place.core, place.y, place.z)
+    own[...] = (merged[...].astype(F32) + stage[1].astype(F32)).astype(BF)
+    for step in (3, 2, 1):
+        sender.send(own, own, base + 2 + place.z, place.device(z=place.layer(step)))
+    for step in range(4):
+        layer = place.layer(step)
+        block = view(place.core, place.y, layer)
+        if step > 0:
+            yield
+            sender.arrived(block, base + 2 + layer)
+        sender.send(block, block, base + 6 + layer, place.over_y)
+        sender.send(block, block, base + 10 + layer, place.sibling)
+    for step in range(4):
+        yield
+        layer = place.layer(step)
+        block = view(place.core, 1 - place.y, layer)
+        sender.arrived(block, base + 6 + layer)
+        sender.send(block, block, base + 14 + layer, place.sibling)
+    yield
+    for step in range(4):
+        layer = place.layer(step)
+        sender.arrived(view(1 - place.core, place.y, layer), base + 10 + layer)
+        sender.arrived(view(1 - place.core, 1 - place.y, layer), base + 14 + layer)
+
+
+def sum_steps(place, sender, base, part_ref, work, stage_core, stage_pair, stage_z, final, stage_last, out_ref):
+    mine = tile(place.core, HALF, HALF)
+    other = tile(1 - place.core, HALF, HALF)
+    blocks = [(dx, dy, z) for z in range(4) for dx, dy in ((1, 1), (1, 0), (0, 1), (0, 0))]
+
+    def rows_of(dx, dy, z):
+        chip = place.chip(1 - place.x if dx else place.x, 1 - place.y if dy else place.y, z)
+        return tile(chip, 2 * OWN, 2 * OWN)
+
+    def add(index, landed):
+        work[index] = (work[index].astype(F32) + landed.astype(F32)).astype(BF)
+
+    for index, (dx, dy, z) in enumerate(blocks):
+        sender.send(part_ref.at[rows_of(dx, dy, z), other], stage_core.at[index], base + index, place.sibling)
+    for index, (dx, dy, z) in enumerate(blocks):
+        if index % 4 == 0:
+            yield
+        sender.arrived(stage_core.at[index], base + index)
+        work[index] = (part_ref[rows_of(dx, dy, z), mine].astype(F32) + stage_core[index].astype(F32)).astype(BF)
+        if (dx if z % 2 == 0 else dy) == 1:
+            sender.send(work.at[index], stage_pair.at[index], base + 16 + index, place.over_x if z % 2 == 0 else place.over_y)
+    for z in range(4):
+        yield
+        for second in (1, 0):
+            keep = (0, second) if z % 2 == 0 else (second, 0)
+            sent = (1, second) if z % 2 == 0 else (second, 1)
+            index, source = blocks.index(keep + (z,)), blocks.index(sent + (z,))
+            sender.arrived(stage_pair.at[source], base + 16 + source)
+            add(index, stage_pair[source])
+            if second:
+                peer = place.over_y if z % 2 == 0 else place.over_x
+                sender.send(work.at[index], stage_pair.at[index], base + 32 + index, peer)
+    first = blocks.index((0, 0, 0))
+    for z in range(4):
+        yield
+        source = blocks.index(((0, 1) if z % 2 == 0 else (1, 0)) + (z,))
+        sender.arrived(stage_pair.at[source], base + 32 + source)
+        add(first + 4 * z, stage_pair[source])
+    for step in (3, 2, 1):
+        layer = place.layer(step)
+        sender.send(work.at[first + layer * 4], stage_z.at[step], base + 48 + step, place.device(z=layer))
+    yield
+    total = work[first + place.z * 4].astype(F32)
+    for step in (1, 2, 3):
+        sender.arrived(stage_z.at[step], base + 48 + step)
+        total = total + stage_z[step].astype(F32)
+    top, low = total[:OWN], total[OWN:]
+    is_first = place.core == 0
+    final[...] = jnp.where(is_first, low, top)
+    sender.send(final, stage_last, base + 52, place.sibling)
+    out_ref[:, mine] = jnp.where(is_first, top, low)
+    yield
+    sender.arrived(stage_last, base + 52)
+    out_ref[:, other] = stage_last[...]
+
+
+def run(steps, count=None):
+    while count is None or count > 0:
+        if next(steps, "end") == "end":
+            return
+        if count is not None:
+            count -= 1
+
+
+def layer_kernel(
+    x_ref, vec_ref, wq_ref, wk_ref, wv_ref, wo_ref, w1_ref, w2_ref, qlen_ref, plen_ref, pos_ref,
+    hidden_ref, igrad_ref, qw_ref, qb_ref, kw_ref, vw_ref, vb_ref, ow_ref, ob_ref, g1_ref, s1_ref, iw_ref, ib_ref,
+    tw_ref, tb_ref, g2_ref, s2_ref,
+    wide, stage, wa, wb, vecs, b1, q_s, k_s, v_s, bias, sel, code,
+    block, merged, cls_stage, cls, n1, inv1, h_low, slope, act, n2, inv2, y_low, d_out, d_branch, sums, sums_b1,
+    q_rows, dq, dkv, part, work, stage_core, stage_pair, stage_z, final, stage_last, summed,
+    send_sems, recv_sems,
+):
+    place = Place()
+    sender = Sender(place, send_sems, recv_sems)
+    is_query = place.x == 0
+    core = place.core
+    scr = n1.at[pl.ds(0, 256), :]
+    hid_blk = y_low.at[pl.ds(0, 256), :]
+
+    cut = WIDTH // 2
+    vec_cols = vec_ref[...].T[:OWN, :].astype(BF)
+    filled = (
+        (wq_ref, 0, WIDTH, 0), (wv_ref, 0, cut, 768), (wk_ref, 0, WIDTH, 1280), (wv_ref, cut, cut, 2048),
+        (wo_ref, 0, WIDTH, 2560), (w1_ref, 0, FF, 3328),
+    )
+    wide[...] = jnp.zeros_like(wide)
+    for ref, start, size, at in filled:
+        wide[pl.ds(0, OWN), pl.ds(at, size)] = ref[:, pl.ds(start, size)]
+    wide[pl.ds(0, OWN), pl.ds(1152, 128)] = vec_cols
+    greet(place)
+
+    begin, along, across, corner, twin = weight_steps(place, sender, wa, wb)
+    offsets = (0, HALF)
+    for chunk in range(2):
+        first = pl.multiple_of((0, 2 * HALF)[chunk] + (1 - core) * PART[chunk], 128)
+        sender.send(
+            wide.at[:, pl.ds(first, PART[chunk])], stage.at[:, pl.ds(offsets[chunk], PART[chunk])], 96 + chunk,
+            place.sibling,
+        )
+    wb[tile(place.index, FF_OWN, FF_OWN), :] = w2_ref[...]
+
+    def assemble(chunk):
+        sender.arrived(stage.at[:, pl.ds(offsets[chunk], PART[chunk])], 96 + chunk)
+        first = pl.multiple_of((0, 2 * HALF)[chunk] + core * PART[chunk], 128)
+        mine = wide[pl.ds(0, OWN), pl.ds(first, PART[chunk])].astype(F32)
+        other = stage[pl.ds(0, OWN), pl.ds(offsets[chunk], PART[chunk])].astype(F32)
+        top, low = jnp.where(core == 0, mine, other), jnp.where(core == 0, other, mine)
+        wa[tile(place.chip(), 2 * OWN, 2 * OWN), pl.ds(first, PART[chunk])] = jnp.concatenate([top, low], 0).astype(BF)
+
+    assemble(0)
+    begin(0)
+    assemble(1)
+    begin(1)
+    begin(2)
+
+    ends, starts = [], []
+    for m in range(MICRO):
+        end = jnp.int32(0)
+        ends.append([])
+        starts.append([])
+        for i in range(QS):
+            length = jnp.where(is_query, qlen_ref[m, i], plen_ref[m, i] if i < PS else 0)
+            starts[m].append(end)
+            end = end + length
+            ends[m].append(end)
+    row_of_key = iota((8, STREAM), 1)
+    row_of_query = iota((STREAM, 128), 0)
+    for m in range(MICRO):
+        key_label = jnp.zeros((8, STREAM), jnp.int32)
+        query_label = jnp.zeros((STREAM, 128), jnp.int32)
+        for end in ends[m]:
+            key_label += (row_of_key >= end).astype(jnp.int32)
+            query_label += (row_of_query >= end).astype(jnp.int32)
+        code[:, pl.ds(m * STREAM, STREAM)] = key_label + m * 64
+        same = query_label[:, :1] == key_label[:1, :]
+        bias[pl.ds(m * STREAM, STREAM), :] = jnp.where(same, 0.0, MASKED).astype(BF)
+
+    def cls_places(rows, offset):
+        at = iota((rows, 128), 0)
+        found = jnp.full((rows, 128), -1, jnp.int32)
+        label = jnp.full((rows, 128), -1, jnp.int32)
+        for m in range(MICRO):
+            for i in range(QS):
+                row = jnp.where(is_query, QS * m + i, MICRO * QS + PS * m + i if i < PS else -1000) + offset
+                found = jnp.where(at == row, m * STREAM + starts[m][i], found)
+                label = jnp.where(at == row, m * 64 + i, label)
+        return found[:, :1], label[:, :1]
+
+    found, unused = cls_places(2 * BLOCK, BLOCK * core)
+    sel[...] = (found == iota((2 * BLOCK, ROWS), 1)).astype(BF)
+    coded = jnp.zeros((2 * BLOCK, 128), jnp.int32)
+    at_row, at_lane = iota((2 * BLOCK, 128), 0), iota((2 * BLOCK, 128), 1)
+    for m in range(MICRO):
+        row = jnp.where(is_query, -1000, BLOCK - MICRO + m) + BLOCK * core
+        for i in range(QS):
+            coded = jnp.where((at_row == row) & (at_lane == i), pos_ref[m, i], coded)
+    row_inputs = dot(sel[...], x_ref[...])
+    block[:, pl.ds(0, WIDTH)] = row_inputs.astype(BF)
+    block[:, pl.ds(0, 128)] = (row_inputs[:, :128] + coded.astype(F32)).astype(BF)
+
+    for stage_steps in (along, across, corner, twin):
+        run(stage_steps(0))
+
+    vecs[...] = wa[:, pl.ds(1152, 128)].astype(F32).T[:16, :]
+    low_at, out_at = iota((FF_OWN, 384), 0), iota((FF_OWN, 384), 1)
+    spread = jnp.zeros((FF_OWN, 384), jnp.bool_)
+    row8, lane8 = iota((8, 384), 0), iota((8, 384), 1)
+    pick = jnp.zeros((8, 384), jnp.bool_)
+    for a in range(4):
+        pick |= (lane8 >= 96 * a + 24 * row8) & (lane8 < 96 * a + 24 * row8 + 24) & (row8 < 4)
+        for j in range(4):
+            spread |= (low_at >= 24 * a) & (low_at < 24 * a + 24) & (out_at - low_at == 72 * a + 24 * j)
+    spread = spread.astype(BF)
+    for t in range(8):
+        found_b1 = dot_tn(wa[pl.ds(FF_OWN * t, FF_OWN), pl.ds(1152, 128)], spread)
+        b1[:, pl.ds(384 * t, 384)] = jnp.sum(jnp.where(pick, found_b1[8:16], 0.0), 0, keepdims=True)
+
+    def vec(i):
+        return vecs[pl.ds(i, 1), :]
+
+    def project(i):
+        rows = tile(i, 256, 256)
+        xb = x_ref[rows, :]
+        q_s[rows, :] = ((dot(xb, wa[:, pl.ds(0, WIDTH)]) + vec(0)).astype(BF).astype(F32) * 0.125).astype(BF)
+        v_s[rows, pl.ds(0, cut)] = (dot(xb, wa[:, pl.ds(WIDTH, cut)]) + vecs[pl.ds(1, 1), pl.ds(0, cut)]).astype(BF)
+        k_s[rows, :] = dot(xb, wa[:, pl.ds(HALF, WIDTH)]).astype(BF)
+        v_s[rows, pl.ds(cut, cut)] = (
+            dot(xb, wa[:, pl.ds(HALF + WIDTH, cut)]) + vecs[pl.ds(1, 1), pl.ds(cut, cut)]
+        ).astype(BF)
+
+    steps = along(1)
+    loop(2, project)
+    run(steps, 1)
+    loop(2, lambda i: project(i + 2))
+    run(steps)
+
+    def attend(pair):
+        cols = pl.ds(128 * pair, 128)
+
+        def unit(i):
+            rows = tile(i, 256, 256)
+            keys = tile(i // 2, STREAM, STREAM)
+            q2 = q_s[rows, cols].astype(F32)
+            low_lanes = iota((256, 128), 1) < 64
+            k2, v2 = k_s[keys, cols], v_s[keys, cols]
+            outs = []
+            for head in range(2):
+                qh = jnp.where(low_lanes if head == 0 else ~low_lanes, q2, 0.0).astype(BF)
+                scores = dot_nt(qh, k2) + bias[rows, :].astype(F32)
+                powers = jnp.exp(scores - jnp.max(scores, -1, keepdims=True))
+                shares = powers * (1.0 / jnp.sum(powers, -1, keepdims=True))
+                outs.append(dot(shares.astype(BF), v2))
+            igrad_ref[rows, cols] = jnp.where(low_lanes, outs[0], outs[1]).astype(BF)
+
+        loop(4, unit)
+
+    steps = across(1)
+    for pair in range(6):
+        attend(pair)
+        run(steps, 1)
+    run(steps)
+
+    block[:, pl.ds(WIDTH, WIDTH)] = dot(sel[...], igrad_ref[...]).astype(BF)
+    steps = cls_steps(place, sender, 98, block, merged, cls_stage, cls)
+    run(steps, 1)
+    run(corner(1))
+    run(steps, 1)
+    run(twin(1))
+    run(along(2))
+    run(steps)
+
+    def cls_first(i):
+        rows = tile(i, 320, 320)
+        at = iota((320, 1), 0) + i * 320
+        group = jnp.zeros((320, 1), jnp.int32)
+        for b in range(1, 16):
+            group += (at >= BLOCK * b).astype(jnp.int32)
+        xin = jnp.where(at - BLOCK * group < BLOCK - MICRO, cls[rows, pl.ds(0, WIDTH)].astype(F32), 0.0)
+        normed, inverse = centre(xin + (dot(cls[rows, pl.ds(WIDTH, WIDTH)], wa[:, pl.ds(2560, WIDTH)]) + vec(2)))
+        n1[rows, :] = normed
+        inv1[rows, :] = inverse
+        h_low[rows, :] = (normed * vec(3) + vec(4)).astype(BF)
+
+    loop(2, cls_first)
+
+    def cls_inner(i):
+        rows = tile(i // 6, 320, 320)
+        cols = tile(i % 6, 512, 512)
+        wcols = pl.ds(pl.multiple_of(3328 + (i % 6) * 512, 128), 512)
+        u = dot(h_low[rows, :], wa[:, wcols]) + b1[:, cols]
+        phi = 0.5 * (1.0 + lax.erf(u * 0.7071067811865476))
+        act[rows, cols] = (u * phi).astype(BF)
+        slope[rows, cols] = (phi + u * jnp.exp(-0.5 * u * u) * 0.3989422804014327).astype(BF)
+
+    loop(6, cls_inner)
+    run(across(2))
+    loop(6, lambda i: cls_inner(i + 6))
+    run(corner(2))
+    run(twin(2))
+
+    def cls_second(i):
+        rows = tile(i, 320, 320)
+        r = h_low[rows, :].astype(F32) + (dot(act[rows, :], wb[...]) + vec(5))
+        normed, inverse = centre(r)
+        n2[rows, :] = normed
+        inv2[rows, :] = inverse
+        y_low[rows, :] = (normed * vec(6) + vec(7)).astype(BF)
+
+    loop(2, cls_second)
+
+    at = iota((CLS, 1), 0)
+    at_col = iota((1, CLS), 1)
+
+    def kinds(index):
+        group = jnp.zeros(index.shape, jnp.int32)
+        for b in range(1, 16):
+            group += (index >= BLOCK * b).astype(jnp.int32)
+        inner = index - BLOCK * group
+        query_m = (inner >= QS).astype(jnp.int32)
+        is_q = inner < MICRO * QS
+        passage_m = (inner >= MICRO * QS + PS).astype(jnp.int32)
+        is_p = (inner >= MICRO * QS) & (inner < MICRO * (QS + PS))
+        return group, inner, is_q, query_m, is_p, passage_m
+
+    group, inner, is_q, query_m, unused, unused = kinds(at)
+    unused, unused, unused, unused, col_p, col_m = kinds(at_col)
+    paired = is_q & col_p & (query_m == col_m)
+    source = (group * BLOCK + (BLOCK - MICRO) + query_m == at_col).astype(BF)
+    codes = dot(source, cls[:, pl.ds(0, 128)])
+    wanted = jnp.sum(jnp.where(iota((CLS, 128), 1) == inner - QS * query_m, codes, 0.0), 1, keepdims=True)
+    wanted = wanted.astype(jnp.int32)
+    target = 20 * wanted + MICRO * QS + PS * query_m - 19 * (wanted & 1)
+    hit = paired & (target == at_col)
+    y_all = y_low[...]
+    logits = jnp.where(paired, dot_nt(y_all, y_all) * WIDTH ** -0.5, MASKED)
+    powers = jnp.where(paired, jnp.exp(logits - jnp.max(logits, -1, keepdims=True)), 0.0)
+    total = jnp.sum(powers, -1, keepdims=True)
+    shares = powers * (1.0 / jnp.where(is_q, total, 1.0))
+    d_logits = ((shares - hit.astype(F32)) * (1.0 / MICRO)).astype(BF)
+    d_y = (dot(d_logits, y_all) + dot_tn(d_logits, y_all)) * WIDTH ** -0.5
+    normed = n2[...]
+    sums[pl.ds(0, 1), :] = jnp.sum(d_y * normed, 0, keepdims=True)
+    sums[pl.ds(1, 1), :] = jnp.sum(d_y, 0, keepdims=True)
+    d_sum = centre_back(d_y * vec(6), normed, inv2[...])
+    n2[...] = d_sum
+    d_out[...] = d_sum.astype(BF)
+    sums[pl.ds(2, 1), :] = jnp.sum(d_out[...].astype(F32), 0, keepdims=True)
+
+    def cls_inner_back(i):
+        cols = tile(i, 512, 512)
+        d_act = dot_nt(d_out[...], wb[cols, :])
+        d_u = (d_act * slope[:, cols].astype(F32)).astype(BF)
+        slope[:, cols] = d_u
+        sums_b1[:, cols] = jnp.sum(d_u.astype(F32), 0, keepdims=True)
+
+    loop(6, cls_inner_back)
+
+    def cls_first_back(i):
+        rows = tile(i, 320, 320)
+        d_hidden = n2[rows, :] + dot_nt(slope[rows, :], wa[:, pl.ds(3328, FF)])
+        normed = n1[rows, :]
+        gains = jnp.sum(d_hidden * normed, 0, keepdims=True)
+        shifts = jnp.sum(d_hidden, 0, keepdims=True)
+        d_sum = centre_back(d_hidden * vec(3), normed, inv1[rows, :])
+        n2[rows, :] = d_sum
+        d_low = d_sum.astype(BF)
+        d_branch[rows, :] = d_low
+        totals = (gains, shifts, jnp.sum(d_low.astype(F32), 0, keepdims=True))
+        for place_in, value in enumerate(totals):
+            line = pl.ds(3 + place_in, 1)
+            sums[line, :] = jnp.where(i == 0, value, sums[line, :] + value)
+
+    loop(2, cls_first_back)
+
+    found, label = cls_places(BLOCK, 0)
+    sel40 = (found == iota((BLOCK, ROWS), 1)).astype(BF)
+    ours = label >= 0
+    q_rows[...] = dot(sel40, q_s[...])
+    x_rows = dot(sel40, x_ref[...]).astype(BF)
+    own_sum = jnp.where(ours, n2[tile(place.batch, BLOCK, BLOCK), :], 0.0)
+    d_att = dot_nt(own_sum.astype(BF), wa[:, pl.ds(2560, WIDTH)]).astype(BF).astype(F32)
+    seen = label == code[pl.ds(0, 1), :]
+    seen2 = jnp.concatenate([seen.astype(F32), seen.astype(F32)], 0) > 0.5
+    low_lanes = iota((BLOCK, 128), 1) < 64
+
+    def both(rows):
+        return jnp.concatenate([jnp.where(low_lanes, rows, 0.0), jnp.where(low_lanes, 0.0, rows)], 0).astype(BF)
+
+    for pair in range(6):
+        cols = pl.ds(128 * pair, 128)
+        q2 = both(q_rows[:, cols])
+        d_a2 = both(d_att[:, 128 * pair : 128 * pair + 128])
+        k2, v2 = k_s[:, cols], v_s[:, cols]
+        scores = jnp.where(seen2, dot_nt(q2, k2), MASKED)
+        powers = jnp.where(seen2, jnp.exp(scores - jnp.max(scores, -1, keepdims=True)), 0.0)
+        total = jnp.sum(powers, -1, keepdims=True)
+        shares = powers * (1.0 / jnp.where(total > 0, total, 1.0))
+        d_shares = dot_nt(d_a2, v2)
+        d_scores = (shares * (d_shares - jnp.sum(d_shares * shares, -1, keepdims=True))).astype(BF)
+        d_q2 = dot(d_scores, k2)
+        dq[:, cols] = (jnp.where(low_lanes, d_q2[:BLOCK], d_q2[BLOCK:]) * 0.125).astype(BF)
+        dkv[:, cols] = dot_tn(d_scores, q2).astype(BF)
+        dkv[:, pl.ds(WIDTH + 128 * pair, 128)] = dot_tn(shares.astype(BF), d_a2).astype(BF)
+
+    part[:, pl.ds(0, WIDTH)] = dot_tn(x_rows, dq[...]).astype(BF)
+
+    def project_back(i):
+        cols = tile(i, 256, 256)
+        out = dot_tn(x_ref[...], dkv[:, cols])
+        part[:, pl.ds(pl.multiple_of(WIDTH + i * 256, 128), 256)] = out.astype(BF)
+
+    loop(6, project_back)
+    line = iota((128, WIDTH), 0)
+    q_line = jnp.sum(dq[...].astype(F32), 0, keepdims=True)
+    v_line = jnp.sum(dkv[:, pl.ds(WIDTH, WIDTH)].astype(F32), 0, keepdims=True)
+    lines = jnp.where(line == 0, q_line, jnp.where(line == 1, v_line, 0.0))
+    part[:, pl.ds(3 * WIDTH, 128)] = lines.T.astype(BF)
+    part[:, pl.ds(3 * WIDTH + 128, 128)] = jnp.zeros((WIDTH, 128), BF)
+
+    steps = sum_steps(place, sender, 116, part, work, stage_core, stage_pair, stage_z, final, stage_last, summed)
+    run(steps, 1)
+
+    def all_rows(i):
+        rows = tile(i, 256, 256)
+        branch = dot(igrad_ref[rows, :], wa[:, pl.ds(2560, WIDTH)]) + vec(2)
+        normed, unused = centre(x_ref[rows, :].astype(F32) + branch)
+        low = (normed * vec(3) + vec(4)).astype(BF)
+        hid_blk[...] = low
+        scr[...] = low.astype(F32) + vec(5)
+
+        def inner_cols(j):
+            cols = tile(j, 512, 512)
+            u = dot(hid_blk[...], wa[:, pl.ds(pl.multiple_of(3328 + j * 512, 128), 512)]) + b1[:, cols]
+            active = (u * (0.5 * (1.0 + lax.erf(u * 0.7071067811865476)))).astype(BF)
+            scr[...] += dot(active, wb[cols, :])
+
+        loop(6, inner_cols)
+        normed, unused = centre(scr[...])
+        last = jnp.where(i < 2, ends[0][QS - 1], ends[1][QS - 1])
+        valid = iota((256, 1), 0) + (i % 2) * 256 < last
+        hidden_ref[rows, :] = jnp.where(valid, normed * vec(6) + vec(7), 0.0).astype(BF)
+
+    for i in range(4):
+        loop(1, lambda j: all_rows(j + i))
+        run(steps, 3)
+
+    back_rows = dot_nt(dq[...], wa[:, pl.ds(0, WIDTH)]) + own_sum
+    q_s[:, pl.ds(0, 128)] = jnp.concatenate([sel40.astype(F32), jnp.zeros((128 - BLOCK, ROWS), F32)], 0).T.astype(BF)
+    back_low = jnp.concatenate([back_rows, jnp.zeros((128 - BLOCK, WIDTH), F32)], 0)
+    back_rest = (back_low - back_low.astype(BF).astype(F32)).astype(BF)
+    back_low = back_low.astype(BF)
+
+    def input_back(i):
+        rows = tile(i, 256, 256)
+        total = dot_nt(dkv[rows, pl.ds(0, WIDTH)], wa[:, pl.ds(HALF, WIDTH)])
+        total += dot_nt(dkv[rows, pl.ds(WIDTH, cut)], wa[:, pl.ds(WIDTH, cut)])
+        total += dot_nt(dkv[rows, pl.ds(WIDTH + cut, cut)], wa[:, pl.ds(HALF + WIDTH, cut)])
+        hit_rows = q_s[rows, pl.ds(0, 128)]
+        total += dot(hit_rows, back_low) + dot(hit_rows, back_rest)
+        igrad_ref[rows, :] = total.astype(BF)
+
+    loop(4, input_back)
+
+    tall_first = jnp.minimum(place.index * FF_OWN // 128, (FF - 256) // 128) * 128
+    tall_at = place.index * FF_OWN - tall_first
+    own_first = jnp.minimum(place.index * OWN // 128, (WIDTH - 256) // 128) * 128
+    own_at = place.index * OWN - own_first
+
+    scr[...] = dot_tn(act[:, pl.ds(pl.multiple_of(tall_first, 128), 256)], d_out[...])
+    tw_ref[...] = scr[pl.ds(pl.multiple_of(tall_at, 8), FF_OWN), :]
+    own_cols = pl.ds(pl.multiple_of(own_first, 128), 256)
+    own_lines = pl.ds(pl.multiple_of(own_at, 8), OWN)
+    att_cols = pl.ds(pl.multiple_of(own_first + WIDTH, 128), 256)
+    scr[...] = dot_tn(cls[:, att_cols], d_branch[...])
+    ow_ref[...] = scr[own_lines, :]
+    for j in range(4):
+        scr[...] = dot_tn(h_low[:, own_cols], slope[:, pl.ds(WIDTH * j, WIDTH)])
+        iw_ref[:, pl.ds(WIDTH * j, WIDTH)] = scr[own_lines, :]
+
+    def own_lanes(line, first, shift, size):
+        window = jnp.broadcast_to(line[:, pl.ds(pl.multiple_of(first, 128), 256)], (8, 256))
+        return pltpu.roll(window, 256 - shift, 1)[:1, :size]
+
+    for ref, i in ((g2_ref, 0), (s2_ref, 1), (tb_ref, 2), (g1_ref, 3), (s1_ref, 4), (ob_ref, 5)):
+        ref[...] = own_lanes(sums.at[pl.ds(i, 1), :], own_first, own_at, OWN)
+    ib_ref[...] = own_lanes(sums_b1, tall_first, tall_at, FF_OWN)
+
+    run(steps)
+    qw_ref[...] = summed[:, pl.ds(0, WIDTH)]
+    kw_ref[...] = summed[:, pl.ds(WIDTH, WIDTH)]
+    vw_ref[...] = summed[:, pl.ds(2 * WIDTH, WIDTH)]
+    lines = jnp.concatenate([summed[:, pl.ds(3 * WIDTH, 128)], jnp.zeros((128 - OWN, 128), F32)], 0).T
+    qb_ref[...] = lines[0:1, :OWN]
+    vb_ref[...] = lines[1:2, :OWN]
+    sender.close()
+
+
+def fast(hidden_in, query_lengths, passage_lengths, positives, stored):
+    (query_weight, query_bias, key_weight, value_weight, value_bias, output_weight, output_bias, first_gain,
+     first_shift, inner_weight, inner_bias, outer_weight, outer_bias, second_gain, second_shift) = stored
+    vectors = jnp.concatenate(
+        [query_bias, value_bias, output_bias, first_gain, first_shift, outer_bias, second_gain, second_shift, inner_bias]
+    ).astype(F32).reshape(12, OWN)
+    vectors = jnp.pad(vectors, ((0, 116), (0, 128 - OWN)))
+    shapes = [
+        ((ROWS, WIDTH), BF), ((ROWS, WIDTH), BF), ((OWN, WIDTH), F32), ((1, OWN), F32), ((OWN, WIDTH), F32),
+        ((OWN, WIDTH), F32), ((1, OWN), F32), ((OWN, WIDTH), F32), ((1, OWN), F32), ((1, OWN), F32), ((1, OWN), F32),
+        ((OWN, FF), F32), ((1, FF_OWN), F32), ((FF_OWN, WIDTH), F32), ((1, OWN), F32), ((1, OWN), F32), ((1, OWN), F32),
+    ]
+    scratch = [
+        pltpu.VMEM((32, 6400), BF), pltpu.VMEM((32, 3200), BF), pltpu.VMEM((WIDTH, 6400), BF), pltpu.VMEM((FF, WIDTH), BF),
+        pltpu.VMEM((16, WIDTH), F32), pltpu.VMEM((1, FF), F32),
+        pltpu.VMEM((ROWS, WIDTH), BF), pltpu.VMEM((ROWS, WIDTH), BF), pltpu.VMEM((ROWS, WIDTH), BF),
+        pltpu.VMEM((ROWS, STREAM), BF), pltpu.VMEM((2 * BLOCK, ROWS), BF), pltpu.VMEM((8, ROWS), jnp.int32),
+        pltpu.VMEM((2 * BLOCK, 2 * WIDTH), BF), pltpu.VMEM((2 * BLOCK, WIDTH), BF), pltpu.VMEM((2, 2 * BLOCK, WIDTH), BF),
+        pltpu.VMEM((CLS, 2 * WIDTH), BF),
+        pltpu.VMEM((CLS, WIDTH), F32), pltpu.VMEM((CLS, 1), F32), pltpu.VMEM((CLS, WIDTH), BF),
+        pltpu.VMEM((CLS, FF), BF), pltpu.VMEM((CLS, FF), BF),
+        pltpu.VMEM((CLS, WIDTH), F32), pltpu.VMEM((CLS, 1), F32), pltpu.VMEM((CLS, WIDTH), BF),
+        pltpu.VMEM((CLS, WIDTH), BF), pltpu.VMEM((CLS, WIDTH), BF),
+        pltpu.VMEM((8, WIDTH), F32), pltpu.VMEM((1, FF), F32),
+        pltpu.VMEM((BLOCK, WIDTH), F32), pltpu.VMEM((BLOCK, WIDTH), BF), pltpu.VMEM((ROWS, 2 * WIDTH), BF),
+        pltpu.VMEM((WIDTH, 2 * HALF), BF),
+        pltpu.VMEM((16, 2 * OWN, HALF), BF), pltpu.VMEM((16, 2 * OWN, HALF), BF), pltpu.VMEM((16, 2 * OWN, HALF), BF),
+        pltpu.VMEM((4, 2 * OWN, HALF), BF), pltpu.VMEM((OWN, HALF), F32), pltpu.VMEM((OWN, HALF), F32),
+        pltpu.VMEM((OWN, 2 * HALF), F32),
+        pltpu.SemaphoreType.DMA((160,)), pltpu.SemaphoreType.DMA((170,)),
+    ]
+    vmem = pl.BlockSpec(memory_space=pltpu.VMEM)
+    smem = pl.BlockSpec(memory_space=pltpu.SMEM)
+    outs = pl.pallas_call(
+        layer_kernel,
+        out_shape=[jax.ShapeDtypeStruct(shape, kind) for shape, kind in shapes],
+        in_specs=[vmem] * 8 + [smem] * 3,
+        out_specs=[vmem] * len(shapes),
+        scratch_shapes=scratch,
+        compiler_params=pltpu.CompilerParams(collective_id=0, has_side_effects=True, vmem_limit_bytes=63 * 2**20),
+    )(
+        hidden_in.reshape(ROWS, WIDTH), vectors, query_weight, key_weight, value_weight, output_weight, inner_weight,
+        outer_weight, query_lengths, passage_lengths, positives,
+    )
+    shape = hidden_in.shape
+    return tuple(
+        out.reshape(shape) if i < 2 else (out.reshape(-1) if out.shape[0] == 1 else out) for i, out in enumerate(outs)
+    )
 
 
 def local(
@@ -262,6 +1017,9 @@
         second_gain,
         second_shift,
     )
+    sizes = (lax.axis_size("tower"), lax.axis_size("batch"), hidden_in.shape, inner_weight.shape)
+    if sizes == (2, 16, (MICRO, 1, STREAM, WIDTH), (OWN, FF)) and query_lengths.shape[1] == QS:
+        return fast(hidden_in, query_lengths, passage_lengths, positives, stored)
     micro = hidden_in.shape[0]
     width = hidden_in.shape[3]
     cls_scale = width ** (-0.5)

time: 1020 us -> 208 us (0.20)
  waiting for transfers between devices: 468 us -> 0 us
  matrix products: 186 us -> 0 us
  Pallas kernels: 0 us -> 184 us
  blocking collectives: 138 us -> 0 us
  local copies, waits for them, and re-layouts: 114 us -> 18.7 us
  other arithmetic: 46.6 us -> 0.64 us
  starting transfers between devices: 22.1 us -> 0 us
  between operations: 18.2 us -> 1.22 us
  loops' own time: 16.6 us -> 0 us
    dot_general x104 -> x0, matrix products: 186 us -> none  [the longest x42 101 us: product(): return jnp.dot(left, right, preferred_element_type=jnp.float32)]
    pallas_call x0 -> x1, Pallas kernels: none -> 184 us  [fast(): pl.pallas_call(layer_kernel, out_shape=[jax.ShapeDtypeStruct(shape, kind)...]
    reduce_scatter x4 -> x0, waiting for transfers between devices: 142 us -> none  [local(): lax.psum_scatter(half_totals, 'batch', scatter_dimension=0, tiled=True)]
    ppermute x21 -> x0, waiting for transfers between devices: 128 us -> none  [partner_2(): lax.ppermute(x, axis, [(i, i ^ 1 << apart) for i in range(lax.axis_size(a...]
    all_gather x6 -> x0, waiting for transfers between devices: 109 us -> none  [the longest x1 53 us: local(): lax.all_gather(query_weight, ('tower', 'batch'), axis=0, tiled=True)]
    unnamed x2 -> x0, blocking collectives: 100 us -> none
    unnamed x16 -> x0, waiting for transfers between devices: 88.9 us -> none
    all_gather x2 -> x0, blocking collectives: 37.8 us -> none  [local(): pooled = lax.all_gather(passage_cls, 'batch', axis=0, tiled=True)]
  transfers between devices with their start and end apart: 34 -> 0, of which waited for: 16 -> 0; matrix products, arithmetic and copies ran while one was open for 26% -> 0% of each run, Pallas kernels for 0% -> 0%
where the time goes in v2:
time: 208 us; the launch traced here: 204 us
  Pallas kernels  184 us (88%)
  local copies, waits for them, and re-layouts  18.7 us (9%)
    pallas_call x1, Pallas kernels, fast(): pl.pallas_call(layer_kernel, out_shape=[jax.ShapeDtypeStruct(shape, kind)...  184 us
    unnamed x49, local copies, waits for them, and re-layouts  12.5 us
    concatenate x1, local copies, waits for them, and re-layouts, fast(): jnp.concatenate([query_bias, value_bias, output_bias, first_gain, first_s...  6.1 us

profile of v2, /device:TPU:0, one launch (start us, length us, event | category | flops | bytes accessed | tf_op | source)
XLA Modules:
  0.0 204.1 jit_solution(14253120682647451275)
XLA Ops:
  0.7 6.1 %concatenate.3 = bf16[288]{0:T(512)(128)(2,1)S(1)} concatenate(bf16[24]{0:T(256)(128)(2,1)} %param.24, bf16[24]{0:T(256)(128)(2,1)} %param.27, bf16[24]{0:T(256)(128)(2,1)} %param.29, bf16[24]{0:T(256)(128)(2,1)} %param.30, bf16[24]{0:T(256)(128)(2,1)} %param.31, bf16[24]{0:T(256)(128)(2,1)} %param.35, bf16[24]{0:T(256)(128)(2,1)} %param.36, bf16[24]{0:T(256)(128)(2,1)} %param.37, ...), dimensions={0} | concatenate | bytes 1152 | tf_op jit(solution)/shard_map/concatenate | solution.py:935
  6.8 0.1 convert_element_type.7
  6.9 0.6 pad_convert_fusion.vec_ref
  7.5 183.5 %shard_map.314 = (bf16[1024,768]{1,0:T(8,128)(2,1)}, bf16[1024,768]{1,0:T(8,128)(2,1)}, f32[24,768]{1,0:T(8,128)}, f32[1,24]{1,0:T(1,128)}, f32[24,768]{1,0:T(8,...) custom-call(bf16[1024,768]{1,0:T(8,128)(2,1)} %bitcast.16, ...), custom_call_target="tpu_custom_call" | custom-call | tf_op jit(solution)/shard_map/pallas_call | solution.py:965
  191.0 2.8 %copy.55 = bf16[2,1,512,768]{3,2,1,0:T(8,128)(2,1)} copy(bf16[2,1,512,768]{3,2,1,0:T(8,128)(2,1)} %bitcast.18) | data formatting | bytes 3145728
  193.9 1.1 copy.56
  195.1 0.6 copy.57
  195.7 0.5 copy.58
  196.2 0.6 copy.59
  196.9 0.0 copy-done.4
  196.9 0.6 copy.60
  197.5 0.5 copy.61
  198.0 0.6 copy.62
  198.7 0.5 copy.63
  199.2 0.5 copy.64
  199.7 0.5 copy.65
  200.2 0.7 copy.66
  200.9 0.5 copy.67
  201.4 0.7 copy.68
  202.1 0.5 copy.69
  202.7 0.0 copy-done.8
  202.7 0.5 copy.70
  203.2 0.0 copy-done.7
  203.2 0.5 copy.71
  (29 shorter events, 0.1 us)
Async XLA Ops:
  191.0 2.8 %copy-start = (bf16[1024,768]{1,0:T(8,128)(2,1)S(1)}, bf16[1024,768]{1,0:T(8,128)(2,1)}, u32[]{:S(2)}) copy-start(bf16[1024,768]{1,0:T(8,128)(2,1)} %get-tuple-element.35) | copy-start | bytes 4718596
  193.8 1.2 copy-start.6
  193.8 1.9 copy-start.15
  193.8 2.4 %copy-start.5 = (f32[24,768]{1,0:T(8,128)S(1)}, f32[24,768]{1,0:T(8,128)}, u32[]{:S(2)}) copy-start(f32[24,768]{1,0:T(8,128)} %get-tuple-element.89) | copy-start | bytes 221188
  193.8 3.0 %copy-start.4 = (f32[24,768]{1,0:T(8,128)S(1)}, f32[24,768]{1,0:T(8,128)}, u32[]{:S(2)}) copy-start(f32[24,768]{1,0:T(8,128)} %get-tuple-element.90) | copy-start | bytes 221188
  193.8 3.7 %copy-start.14 = (f32[1,24]{1,0:T(1,128)S(1)}, f32[1,24]{1,0:T(1,128)}, u32[]{:S(2)}) copy-start(f32[1,24]{1,0:T(1,128)} %get-tuple-element.40) | copy-start | bytes 292
  193.9 4.2 %copy-start.3 = (f32[24,768]{1,0:T(8,128)S(1)}, f32[24,768]{1,0:T(8,128)}, u32[]{:S(2)}) copy-start(f32[24,768]{1,0:T(8,128)} %get-tuple-element.92) | copy-start | bytes 221188
  193.9 4.8 %copy-start.13 = (f32[1,24]{1,0:T(1,128)S(1)}, f32[1,24]{1,0:T(1,128)}, u32[]{:S(2)}) copy-start(f32[1,24]{1,0:T(1,128)} %get-tuple-element.42) | copy-start | bytes 292
  193.9 5.3 %copy-start.12 = (f32[1,24]{1,0:T(1,128)S(1)}, f32[1,24]{1,0:T(1,128)}, u32[]{:S(2)}) copy-start(f32[1,24]{1,0:T(1,128)} %get-tuple-element.43) | copy-start | bytes 292
  193.9 5.8 %copy-start.11 = (f32[1,24]{1,0:T(1,128)S(1)}, f32[1,24]{1,0:T(1,128)}, u32[]{:S(2)}) copy-start(f32[1,24]{1,0:T(1,128)} %get-tuple-element.44) | copy-start | bytes 292
  193.9 6.3 %copy-start.2 = (f32[24,3072]{1,0:T(8,128)S(1)}, f32[24,3072]{1,0:T(8,128)}, u32[]{:S(2)}) copy-start(f32[24,3072]{1,0:T(8,128)} %get-tuple-element.96) | copy-start | bytes 884740
  193.9 7.0 %copy-start.10 = (f32[1,96]{1,0:T(1,128)S(1)}, f32[1,96]{1,0:T(1,128)}, u32[]{:S(2)}) copy-start(f32[1,96]{1,0:T(1,128)} %get-tuple-element.46) | copy-start | bytes 1156
  193.9 7.5 %copy-start.1 = (f32[96,768]{1,0:T(8,128)S(1)}, f32[96,768]{1,0:T(8,128)}, u32[]{:S(2)}) copy-start(f32[96,768]{1,0:T(8,128)} %get-tuple-element.98) | copy-start | bytes 884740
  195.1 7.1 %copy-start.9 = (f32[1,24]{1,0:T(1,128)S(1)}, f32[1,24]{1,0:T(1,128)}, u32[]{:S(2)}) copy-start(f32[1,24]{1,0:T(1,128)} %get-tuple-element.48) | copy-start | bytes 292
  195.1 7.6 %copy-start.8 = (f32[1,24]{1,0:T(1,128)S(1)}, f32[1,24]{1,0:T(1,128)}, u32[]{:S(2)}) copy-start(f32[1,24]{1,0:T(1,128)} %get-tuple-element.49) | copy-start | bytes 292
  195.1 8.1 %copy-start.7 = (f32[1,24]{1,0:T(1,128)S(1)}, f32[1,24]{1,0:T(1,128)}, u32[]{:S(2)}) copy-start(f32[1,24]{1,0:T(1,128)} %get-tuple-element.50) | copy-start | bytes 292
